TPU v7x, 32 devices: a whole 2x2x4 slice. The times are simulated.
32 devices in a mesh: dp: 16 (over z, y, core), tile: 2 (over x).
Axes of the slice: x: 2, y: 2, z: 4, core: 2. Of those that a mesh axis runs over, the one named last changes fastest.
Arguments:
- fields: bfloat16 [16, 48, 16, 1024], P('dp', 'tile'), may hold values from -6 to 6
- weights: bfloat16 [64, 16, 3, 3], replicated, may hold values from -0.5 to 0.5
- bias: float32 [64], replicated, may hold values from -1 to 1
- cotangent: bfloat16 [16, 48, 64, 1024], P('dp', 'tile'), may hold values from -6 to 6
- neighbours: int32 [48, 8], replicated, may hold values from 0 to 47
- rotations: int32 [48, 8], replicated, may hold values from 0 to 3
- tile_map: int32 [48], replicated, may hold values from 0 to 47, each once
Outputs:
- outputs: bfloat16 [16, 48, 64, 1024], P('dp', 'tile')
- grad_fields: bfloat16 [16, 48, 16, 1024], P('dp', 'tile')
- grad_weights: float32 [64, 16, 3, 3], replicated
- grad_bias: float32 [64], replicated
Inputs may be any that keep to these rules, and one draw needn't show every extreme that they name: neighbours[t, k] is the tile across edge k of tile t (above, below, left, right) for k < 4, and at corner k - 4 (above left, above right, below left, below right) otherwise. `rotations`: counterclockwise quarter turns of the neighbour's tile as seen from tile t. Slot s of the tiled arrays holds tile tile_map[s]; every tile once; device i of tile holds slots i * 24 to (i + 1) * 24 - 1.
All inputs are finite; a program needn't handle non-finite values.
Results may differ from a plain program's by a relative error of at most 0.002.
Values may be sent and summed in bfloat16 or wider, within the bound.
A program may use at most 128 MiB of HBM per device.

v0:
```python
import math

import jax
import jax.numpy as jnp
import numpy as np
from jax import lax
from jax.sharding import PartitionSpec as P

TS = 32


edge_table = np.array(
    [
        [1, 2, 0, 3],
        [0, 3, 1, 2],
        [3, 1, 2, 0],
        [2, 0, 3, 1],
        [1, 1, 0, 0],
        [1, 0, 0, 1],
        [0, 1, 1, 0],
        [0, 0, 1, 1],
    ],
    dtype=np.int32,
)
flip_table = np.array(
    [
        [0, 0, 1, 1],
        [0, 0, 1, 1],
        [0, 1, 1, 0],
        [0, 1, 1, 0],
        [1, 0, 0, 1],
        [0, 0, 1, 1],
        [1, 1, 0, 0],
        [0, 1, 1, 0],
    ],
    dtype=np.int32,
)


def for_sending(x):
    return jax.tree.map(lambda a: a.astype(jnp.bfloat16) if a.dtype == jnp.float32 else a, x)


def slot_tables(tile_map, neighbours, rotations):
    total_slots = tile_map.shape[0]
    places = jnp.arange(total_slots, dtype=jnp.int32)
    onehot = (tile_map[:, None] == places[None, :]).astype(jnp.int32)
    inverse = jnp.sum(
        (tile_map[None, :] == places[:, None]).astype(jnp.int32) * places[None, :], axis=1
    )
    tile_nbr = jnp.sum(onehot[:, :, None] * neighbours[None], axis=1)
    tile_rot = jnp.sum(onehot[:, :, None] * rotations[None], axis=1)
    slot_nbr = jnp.sum(
        (tile_nbr[:, :, None] == places[None, None, :]).astype(jnp.int32) * inverse[None, None, :],
        axis=2,
    )
    matches = (tile_rot[:, :, None] == jnp.arange(4, dtype=jnp.int32)).astype(jnp.int32)
    edge_code = jnp.sum(matches * jnp.asarray(edge_table)[None], axis=-1)
    flip_code = jnp.sum(matches * jnp.asarray(flip_table)[None], axis=-1)
    return (slot_nbr, edge_code, flip_code)


def edges_of(field):
    return jnp.stack(
        [field[..., 0, :], field[..., -1, :], field[..., :, 0], field[..., :, -1]], axis=3
    )


def flipped(values, flags):
    return jnp.where(flags[None, :, :, None, None] == 1, values[..., ::-1], values)


def corner_strips(values, tile_side):
    padding = jnp.zeros(values.shape + (tile_side - 1,), values.dtype)
    return jnp.concatenate([values[..., None], padding], axis=-1)


def body(fields, weights, bias, cotangent, neighbours, rotations, tile_map):
    batch_loc, slot_count, in_chans, _ = fields.shape
    tile_side = TS
    out_chans = weights.shape[0]
    fields = fields.reshape(batch_loc, slot_count, in_chans, tile_side, tile_side)
    cotangent = cotangent.reshape(batch_loc, slot_count, out_chans, tile_side, tile_side)
    slot_nbr, edge_code, flip_code = slot_tables(tile_map, neighbours, rotations)
    base_slot = lax.axis_index("tile") * slot_count
    own_nbr = lax.dynamic_slice_in_dim(slot_nbr, base_slot, slot_count, 0)
    own_edge = lax.dynamic_slice_in_dim(edge_code, base_slot, slot_count, 0)
    own_flip = lax.dynamic_slice_in_dim(flip_code, base_slot, slot_count, 0)
    own_slot = base_slot + jnp.arange(slot_count, dtype=jnp.int32)
    four_edges = jnp.arange(4, dtype=jnp.int32)
    portion = lax.all_gather(edges_of(fields), "tile", axis=1, tiled=True)
    sources = jnp.arange(portion.shape[1], dtype=jnp.int32)
    chosen = (
        (own_nbr[:, :, None, None] == sources[None, None, :, None])
        & (own_edge[:, :, None, None] == four_edges[None, None, None, :])
    ).astype(jnp.bfloat16)
    picked = jnp.einsum("jkqe,bqcet->bjkct", chosen, portion, preferred_element_type=jnp.float32)
    rims = flipped(picked, own_flip).astype(jnp.bfloat16)
    tips = rims[:, :, 4:, :, 0]
    top_row = jnp.concatenate(
        [tips[:, :, 0, :, None], rims[:, :, 0], tips[:, :, 1, :, None]], axis=-1
    )
    low_row = jnp.concatenate(
        [tips[:, :, 2, :, None], rims[:, :, 1], tips[:, :, 3, :, None]], axis=-1
    )
    middle = jnp.concatenate(
        [rims[:, :, 2, :, :, None], fields, rims[:, :, 3, :, :, None]], axis=-1
    )
    padded = jnp.concatenate([top_row[..., None, :], middle, low_row[..., None, :]], axis=-2)
    stacked_tiles = padded.reshape(batch_loc * slot_count, in_chans, tile_side + 2, tile_side + 2)
    response = lax.conv_general_dilated(
        stacked_tiles,
        weights,
        (1, 1),
        "VALID",
        dimension_numbers=("NCHW", "OIHW", "NCHW"),
        preferred_element_type=jnp.float32,
    )
    outputs = (response + bias[None, :, None, None]).astype(jnp.bfloat16)
    outputs = outputs.reshape(batch_loc, slot_count, out_chans, tile_side * tile_side)
    cot_flat = cotangent.reshape(batch_loc * slot_count, out_chans, tile_side, tile_side)
    kernel_taps = []
    for row_tap in range(3):
        kernel_taps.append(
            jnp.stack(
                [
                    jnp.einsum(
                        "nihw,nohw->oi",
                        stacked_tiles[
                            :, :, row_tap : row_tap + tile_side, col_tap : col_tap + tile_side
                        ],
                        cot_flat,
                        preferred_element_type=jnp.float32,
                    )
                    for col_tap in range(3)
                ],
                axis=-1,
            )
        )
    kernel_sum = jnp.stack(kernel_taps, axis=-2)
    bias_sum = jnp.sum(cotangent, axis=(0, 1, 3, 4), dtype=jnp.float32)
    factor = 1.0 / math.sqrt(
        batch_loc * lax.axis_size("dp") * slot_count * lax.axis_size("tile") * tile_side * tile_side
    )
    grad_weights, grad_bias = lax.psum((kernel_sum * factor, bias_sum * factor), ("dp", "tile"))
    turned = jnp.flip(weights, (2, 3)).transpose(1, 0, 2, 3)
    start_back = jnp.zeros((batch_loc, slot_count, 4, in_chans, tile_side), jnp.float32)
    spread = lax.conv_general_dilated(
        cot_flat,
        turned,
        (1, 1),
        ((2, 2), (2, 2)),
        dimension_numbers=("NCHW", "OIHW", "NCHW"),
        preferred_element_type=jnp.float32,
    )
    spread = spread.reshape(batch_loc, slot_count, in_chans, tile_side + 2, tile_side + 2)
    inner = spread[..., 1:-1, 1:-1]
    edge_cot = jnp.stack(
        [spread[..., 0, 1:-1], spread[..., -1, 1:-1], spread[..., 1:-1, 0], spread[..., 1:-1, -1]],
        axis=2,
    )
    corner_cot = jnp.stack(
        [spread[..., 0, 0], spread[..., 0, -1], spread[..., -1, 0], spread[..., -1, -1]], axis=2
    )
    edge_sent = flipped(edge_cot, own_flip[:, :4])
    portion = (
        lax.all_gather(for_sending(edge_sent), "tile", axis=1, tiled=True),
        lax.all_gather(corner_cot.astype(jnp.bfloat16), "tile", axis=1, tiled=True).astype(
            jnp.float32
        ),
    )
    offset = jnp.int32(0)
    edge_vals = portion[0]
    src_flip = lax.dynamic_slice_in_dim(flip_code, offset, edge_vals.shape[1], 0)
    strips = flipped(corner_strips(portion[1], edge_vals.shape[-1]), src_flip[:, 4:])
    portion = jnp.concatenate([edge_vals, strips], axis=2)
    span_rows = portion.shape[1]
    src_nbr = lax.dynamic_slice_in_dim(slot_nbr, offset, span_rows, 0)
    src_edge = lax.dynamic_slice_in_dim(edge_code, offset, span_rows, 0)
    targets = (
        (src_nbr[None, None] == own_slot[:, None, None, None])
        & (src_edge[None, None] == four_edges[None, :, None, None])
    ).astype(jnp.float32)
    arrived = start_back + jnp.einsum(
        "jeqk,bqkct->bject", targets, portion, precision=lax.Precision.HIGHEST
    )
    inner = inner.at[..., 0, :].add(arrived[:, :, 0])
    inner = inner.at[..., -1, :].add(arrived[:, :, 1])
    inner = inner.at[..., :, 0].add(arrived[:, :, 2])
    inner = inner.at[..., :, -1].add(arrived[:, :, 3])
    grad_fields = inner.astype(jnp.bfloat16).reshape(
        batch_loc, slot_count, in_chans, tile_side * tile_side
    )
    return (outputs, grad_fields, grad_weights, grad_bias)


def solution(mesh):
    placed = (P("dp", "tile", None, None), P(), P(), P("dp", "tile", None, None), P(), P(), P())
    return jax.shard_map(
        body,
        mesh=mesh,
        in_specs=placed,
        out_specs=(P("dp", "tile", None, None), P("dp", "tile", None, None), P(), P()),
        check_vma=False,
    )
```

profile of v0, /device:TPU:0, one launch (start us, length us, event | category | flops | bytes accessed | tf_op | source)
XLA Modules:
  0.0 428.4 jit_solution(17076461958220035394)
XLA Ops:
  11.8 3.8 reshape.346
  15.6 4.2 slice_reduce_fusion.1
  21.6 12.9 %all_gather.9 = bf16[1,48,16,4,32]{4,2,3,0,1:T(8,128)(2,1)S(1)} all-gather(bf16[1,24,16,4,32]{4,2,3,0,1:T(8,128)(2,1)S(1)} %copy.620), channel_id=1, replica_groups=mesh['dp'=16,'tile'=2] {'tile'}, dimensions={1}, use_global_device_ids=true | all-gather | bytes 294912 | tf_op jit(solution)/shard_map/all_gather | solution.py:91
  53.2 6.5 %copy.627 = bf16[1,24,16,32,32]{1,2,4,3,0:T(8,128)(2,1)} copy(bf16[1,24,16,32,32]{4,3,2,1,0:T(8,128)(2,1)S(1)} %reshape.346) | data formatting | bytes 1572864 | tf_op jit(solution)/shard_map/reshape | solution.py:82
  59.7 15.0 %add_convert_fusion = bf16[24,64,32,32]{1,0,3,2:T(8,128)(2,1)} fusion(f32[64]{0:T(128)S(1)} %copy-done.11, bf16[64,16,3,3]{0,1,3,2:T(8,128)(2,1)S(1)} %copy-done, bf16[1,24,16,1,34]{1,2,4,3,0:T(8,128)(2,1)S(1)} %copy.633, bf16[1,24,16,32,1]{1,2,4,3,0:T(8,128)(2,1)} %copy.628, bf16[1,24,16,32,32]{1,2,4,3,0:T(8,128)(2,1)} %copy.627, ...), kind=kOutput, calls=%fused_computation | convolution fusion | flops 457906176 | bytes 4052224 | tf_op jit(solution)/shard_map/conv_general_dilated | solution.py:111
  74.7 7.8 %copy.666 = bf16[1,24,64,1024]{3,2,1,0:T(8,128)(2,1)} copy(bf16[1,24,64,1024]{2,1,3,0:T(8,128)(2,1)} %bitcast.223) | data formatting | bytes 6291456
  82.5 6.2 %copy.683 = bf16[1,24,64,1024]{2,1,3,0:T(8,128)(2,1)} copy(bf16[1,24,64,1024]{3,2,1,0:T(8,128)(2,1)S(1)} %copy-done.1) | data formatting | bytes 6291456 | tf_op jit(solution)/shard_map/reshape;reshape | solution.py:121
  88.7 11.8 %convolution_bitcast_fusion.1 = f32[64,16,1]{0,1,2:T(8,128)S(1)} fusion(bf16[24,64,32,32]{1,0,3,2:T(8,128)(2,1)} %bitcast.213, bf16[1,24,16,1,34]{1,2,4,3,0:T(8,128)(2,1)S(1)} %copy.633, bf16[1,24,16,32,1]{1,2,4,3,0:T(8,128)(2,1)} %copy.628, bf16[1,24,16,32,32]{1,2,4,3,0:T(8,128)(2,1)} %copy.627, bf16[1,24,16,32,1]{1,2,4,3,0:T(8,128)(2,1)} %copy.626, ...), kind=kOutput, calls=%fused_computation.14 | convolution fusion | flops 54770688 | bytes 4037632 | tf_op jit(solution)/shard_map/nihw,nohw->oi/dot_general | solution.py:127
  100.6 4.5 %convolution_bitcast_fusion.2 = f32[64,16,1]{0,1,2:T(8,128)S(1)} fusion(bf16[24,64,32,32]{1,0,3,2:T(8,128)(2,1)S(1)} %bitcast.215, bf16[1,24,16,1,34]{1,2,4,3,0:T(8,128)(2,1)S(1)} %copy.633, bf16[1,24,16,32,1]{1,2,4,3,0:T(8,128)(2,1)S(1)} %copy-done.5, bf16[1,24,16,32,32]{1,2,4,3,0:T(8,128)(2,1)S(1)} %copy-done.3, ...), kind=kOutput, calls=%fused_computation.15 | convolution fusion | flops 54770688 | bytes 4037632 | tf_op jit(solution)/shard_map/nihw,nohw->oi/dot_general | solution.py:127
  105.1 4.5 %convolution_bitcast_fusion.3 = f32[64,16,1]{0,1,2:T(8,128)S(1)} fusion(bf16[24,64,32,32]{1,0,3,2:T(8,128)(2,1)S(1)} %bitcast.216, bf16[1,24,16,1,34]{1,2,4,3,0:T(8,128)(2,1)S(1)} %copy.633, bf16[1,24,16,32,1]{1,2,4,3,0:T(8,128)(2,1)S(1)} %copy-done.5, bf16[1,24,16,32,32]{1,2,4,3,0:T(8,128)(2,1)S(1)} %copy-done.3, ...), kind=kOutput, calls=%fused_computation.16 | convolution fusion | flops 54770688 | bytes 4037632 | tf_op jit(solution)/shard_map/nihw,nohw->oi/dot_general | solution.py:127
  109.7 4.5 %convolution_bitcast_fusion.4 = f32[64,16,1]{0,1,2:T(8,128)S(1)} fusion(bf16[24,64,32,32]{1,0,3,2:T(8,128)(2,1)S(1)} %bitcast.217, bf16[1,24,16,1,34]{1,2,4,3,0:T(8,128)(2,1)S(1)} %copy.633, bf16[1,24,16,32,1]{1,2,4,3,0:T(8,128)(2,1)S(1)} %copy-done.5, bf16[1,24,16,32,32]{1,2,4,3,0:T(8,128)(2,1)S(1)} %copy-done.3, ...), kind=kOutput, calls=%fused_computation.17 | convolution fusion | flops 54770688 | bytes 4037632 | tf_op jit(solution)/shard_map/nihw,nohw->oi/dot_general | solution.py:127
  114.2 4.7 %convolution_bitcast_fusion.5 = f32[64,16,1]{0,1,2:T(8,128)S(1)} fusion(bf16[24,64,32,32]{1,0,3,2:T(8,128)(2,1)S(1)} %bitcast.218, bf16[1,24,16,1,34]{1,2,4,3,0:T(8,128)(2,1)S(1)} %copy.633, bf16[1,24,16,32,1]{1,2,4,3,0:T(8,128)(2,1)S(1)} %copy-done.5, bf16[1,24,16,32,32]{1,2,4,3,0:T(8,128)(2,1)S(1)} %copy-done.3, ...), kind=kOutput, calls=%fused_computation.18 | convolution fusion | flops 54770688 | bytes 4037632 | tf_op jit(solution)/shard_map/nihw,nohw->oi/dot_general | solution.py:127
  119.0 4.5 %convolution_bitcast_fusion.6 = f32[64,16,1]{0,1,2:T(8,128)S(1)} fusion(bf16[24,64,32,32]{1,0,3,2:T(8,128)(2,1)S(1)} %bitcast.219, bf16[1,24,16,1,34]{1,2,4,3,0:T(8,128)(2,1)S(1)} %copy.633, bf16[1,24,16,32,1]{1,2,4,3,0:T(8,128)(2,1)S(1)} %copy-done.5, bf16[1,24,16,32,32]{1,2,4,3,0:T(8,128)(2,1)S(1)} %copy-done.3, ...), kind=kOutput, calls=%fused_computation.19 | convolution fusion | flops 54770688 | bytes 4037632 | tf_op jit(solution)/shard_map/nihw,nohw->oi/dot_general | solution.py:127
  123.5 4.5 %convolution_bitcast_fusion.7 = f32[64,16,1]{0,1,2:T(8,128)S(1)} fusion(bf16[24,64,32,32]{1,0,3,2:T(8,128)(2,1)S(1)} %bitcast.220, bf16[1,24,16,1,34]{1,2,4,3,0:T(8,128)(2,1)S(1)} %copy.633, bf16[1,24,16,32,1]{1,2,4,3,0:T(8,128)(2,1)S(1)} %copy-done.5, bf16[1,24,16,32,32]{1,2,4,3,0:T(8,128)(2,1)S(1)} %copy-done.3, ...), kind=kOutput, calls=%fused_computation.20 | convolution fusion | flops 54770688 | bytes 4037632 | tf_op jit(solution)/shard_map/nihw,nohw->oi/dot_general | solution.py:127
  128.1 4.6 %convolution_bitcast_fusion.8 = f32[64,16,1]{0,1,2:T(8,128)S(1)} fusion(bf16[24,64,32,32]{1,0,3,2:T(8,128)(2,1)S(1)} %bitcast.221, bf16[1,24,16,1,34]{1,2,4,3,0:T(8,128)(2,1)S(1)} %copy.633, bf16[1,24,16,32,1]{1,2,4,3,0:T(8,128)(2,1)S(1)} %copy-done.5, bf16[1,24,16,32,32]{1,2,4,3,0:T(8,128)(2,1)S(1)} %copy-done.3, ...), kind=kOutput, calls=%fused_computation.21 | convolution fusion | flops 54770688 | bytes 4037632 | tf_op jit(solution)/shard_map/nihw,nohw->oi/dot_general | solution.py:127
  132.6 4.7 %convolution_bitcast_fusion.9 = f32[64,16,1]{0,1,2:T(8,128)S(1)} fusion(bf16[24,64,32,32]{1,0,3,2:T(8,128)(2,1)S(1)} %bitcast.222, bf16[1,24,16,1,34]{1,2,4,3,0:T(8,128)(2,1)S(1)} %copy.633, bf16[1,24,16,32,1]{1,2,4,3,0:T(8,128)(2,1)S(1)} %copy-done.5, bf16[1,24,16,32,32]{1,2,4,3,0:T(8,128)(2,1)S(1)} %copy-done.3, ...), kind=kOutput, calls=%fused_computation.22 | convolution fusion | flops 54770688 | bytes 4037632 | tf_op jit(solution)/shard_map/nihw,nohw->oi/dot_general | solution.py:127
  137.4 42.1 %all-reduce.1 = (f32[64,16,3,3]{0,1,3,2:T(8,128)}, f32[64]{0:T(128)}) all-reduce(f32[64,16,3,3]{0,1,3,2:T(8,128)S(1)} %maximum_multiply_fusion, f32[64]{0:T(128)S(1)} %broadcast_multiply_fusion), channel_id=1, replica_groups=mesh['dp'=16,'tile'=2] {'dp','tile'}, use_global_device_ids=true, to_apply=%region_6.7 | all-reduce | flops 9280 | bytes 74240 | tf_op jit(solution)/shard_map/psum | solution.py:145
  179.5 61.8 %fusion.24 = f32[24,16,34,34]{0,1,3,2:T(8,128)} fusion(bf16[24,64,32,32]{1,0,3,2:T(8,128)(2,1)} %bitcast.214, bf16[64,16,3,3]{0,1,3,2:T(8,128)(2,1)S(1)} %copy-done), kind=kOutput, calls=%fused_computation.91 | convolution fusion | flops 452984832 | bytes 4939776 | tf_op jit(solution)/shard_map/conv_general_dilated | solution.py:148
  241.3 10.9 %copy.636 = f32[24,16,34,34]{2,1,0,3:T(8,128)} copy(f32[24,16,34,34]{0,1,3,2:T(8,128)} %fusion.24) | data formatting | bytes 3551232 | tf_op jit(solution)/shard_map/conv_general_dilated | solution.py:148
  258.5 5.1 %all_gather.11 = bf16[1,48,4,16]{3,2,0,1:T(4,128)(2,1)S(1)} all-gather(bf16[1,24,4,16]{3,2,0,1:T(4,128)(2,1)S(1)} %copy.649), channel_id=1, replica_groups=mesh['dp'=16,'tile'=2] {'tile'}, dimensions={1}, use_global_device_ids=true | all-gather | bytes 9216 | tf_op jit(solution)/shard_map/all_gather | solution.py:168
  264.9 7.7 %slice.298 = f32[1,24,16,32,32]{3,2,1,4,0:T(8,128)} slice(f32[1,24,16,34,34]{3,2,1,4,0:T(8,128)} %bitcast.208), slice={[0:1], [0:24], [0:16], [1:33], [1:33]} | slice | bytes 3145728 | tf_op jit(solution)/shard_map/slice | solution.py:157
  276.0 4.7 %copy.638 = bf16[1,24,16,1,32]{4,2,1,3,0:T(8,128)(2,1)S(1)} copy(bf16[1,24,16,1,32]{3,2,1,4,0:T(8,128)(2,1)} %get-tuple-element.126) | data formatting | bytes 49152 | tf_op jit(solution)/shard_map/slice | solution.py:159
  286.9 9.4 %all_gather.10 = bf16[1,48,4,16,32]{4,3,2,0,1:T(8,128)(2,1)S(1)} all-gather(bf16[1,24,4,16,32]{4,3,2,0,1:T(8,128)(2,1)S(1)} %fusion.5), channel_id=1, replica_groups=mesh['dp'=16,'tile'=2] {'tile'}, dimensions={1}, use_global_device_ids=true | all-gather | bytes 294912 | tf_op jit(solution)/shard_map/all_gather | solution.py:167
  300.5 6.4 %copy.653 = f32[1,24,16,1,32]{3,2,1,4,0:T(8,128)} copy(f32[1,24,16,1,32]{4,2,1,3,0:T(8,128)S(1)} %slice_bitcast_fusion.3) | data formatting | bytes 98304 | tf_op jit(solution)/shard_map/reshape.106
  306.8 9.0 %slice_add_fusion = f32[1,24,16,1,32]{3,2,1,4,0:T(8,128)} fusion(f32[1,24,16,1,32]{3,2,1,4,0:T(8,128)} %copy.653, f32[1,24,16,34,34]{3,2,1,4,0:T(8,128)} %bitcast.209), kind=kLoop, calls=%fused_computation.1 | loop fusion | flops 12288 | bytes 147456 | tf_op jit(solution)/shard_map/add | solution.py:187
  315.8 14.7 %scatter-add.14 = f32[1,24,16,32,32]{3,2,1,4,0:T(8,128)} dynamic-update-slice(f32[1,24,16,32,32]{3,2,1,4,0:T(8,128)} %slice.298, f32[1,24,16,1,32]{3,2,1,4,0:T(8,128)} %slice_add_fusion, s32[]{:T(128)} %constant.126.clone.1, s32[]{:T(128)} %constant.126.clone.1, s32[]{:T(128)} %constant.126.clone.1, s32[]{:T(128)} %constant.126.clone.1, s32[]{:T(128)} %constant.126.clone.1) | dynamic-update-slice | bytes 98308 | tf_op jit(solution)/shard_map/scatter-add | solution.py:187
  330.5 7.1 %slice.309 = f32[1,24,16,1,32]{3,2,1,4,0:T(8,128)} slice(f32[1,24,16,32,32]{3,2,1,4,0:T(8,128)} %scatter-add.14), slice={[0:1], [0:24], [0:16], [31:32], [0:32]} | slice | bytes 98304 | tf_op jit(solution)/shard_map/slice.154
  337.6 5.2 %copy.693 = f32[1,24,16,1,32]{4,2,1,3,0:T(8,128)S(1)} copy(f32[1,24,16,1,32]{3,2,1,4,0:T(8,128)} %slice.309) | data formatting | bytes 98304
  342.9 6.2 %copy.655 = f32[1,24,16,1,32]{3,2,1,4,0:T(8,128)} copy(f32[1,24,16,1,32]{4,2,1,3,0:T(8,128)S(1)} %fusion.14) | data formatting | bytes 98304 | tf_op jit(solution)/shard_map/add | solution.py:188
  349.0 62.8 %scatter-add.15 = f32[1,24,16,32,32]{3,2,1,4,0:T(8,128)} dynamic-update-slice(f32[1,24,16,32,32]{3,2,1,4,0:T(8,128)} %scatter-add.14, f32[1,24,16,1,32]{3,2,1,4,0:T(8,128)} %copy.655, s32[]{:T(128)} %constant.126.clone.1, s32[]{:T(128)} %constant.126.clone.1, s32[]{:T(128)} %constant.126.clone.1, s32[]{:T(128)} %constant.132.clone.1, s32[]{:T(128)} %constant.126.clone.1) | dynamic-update-slice | bytes 98308 | tf_op jit(solution)/shard_map/scatter-add | solution.py:188
  418.5 4.2 copy.656
  422.7 5.6 %reshape.356 = bf16[1,24,16,1024]{3,2,1,0:T(8,128)(2,1)} reshape(bf16[1,24,16,32,32]{4,3,2,1,0:T(8,128)(2,1)} %copy.656) | data formatting | bytes 1572864 | tf_op jit(solution)/shard_map/reshape | solution.py:191
  (101 shorter events, 59.5 us)
Async XLA Ops:
  0.6 59.0 %copy-start = (bf16[64,16,3,3]{0,1,3,2:T(8,128)(2,1)S(1)}, bf16[64,16,3,3]{0,1,3,2:T(8,128)(2,1)}, u32[]{:S(2)}) copy-start(bf16[64,16,3,3]{0,1,3,2:T(8,128)(2,1)} %param.18) | copy-start | bytes 55300
  41.2 18.5 %copy-start.11 = (f32[64]{0:T(128)S(1)}, f32[64]{0:T(128)}, u32[]{:S(2)}) copy-start(f32[64]{0:T(128)} %param.19) | copy-start | bytes 772
  74.7 7.8 %copy-start.1 = (bf16[1,24,64,1024]{3,2,1,0:T(8,128)(2,1)S(1)}, bf16[1,24,64,1024]{3,2,1,0:T(8,128)(2,1)}, u32[]{:S(2)}) copy-start(bf16[1,24,64,1024]{3,2,1,0:T(8,128)(2,1)} %param.20) | copy-start | bytes 9437188
  88.7 11.8 %copy-start.2 = (bf16[1,24,64,1024]{2,1,3,0:T(8,128)(2,1)S(1)}, bf16[1,24,64,1024]{2,1,3,0:T(8,128)(2,1)}, u32[]{:S(2)}) copy-start(bf16[1,24,64,1024]{2,1,3,0:T(8,128)(2,1)} %copy.683) | copy-start | bytes 9437188
  88.7 11.8 %copy-start.3 = (bf16[1,24,16,32,32]{1,2,4,3,0:T(8,128)(2,1)S(1)}, bf16[1,24,16,32,32]{1,2,4,3,0:T(8,128)(2,1)}, u32[]{:S(2)}) copy-start(bf16[1,24,16,32,32]{1,2,4,3,0:T(8,128)(2,1)} %copy.627) | copy-start | bytes 2359300
  88.7 11.8 %copy-start.5 = (bf16[1,24,16,32,1]{1,2,4,3,0:T(8,128)(2,1)S(1)}, bf16[1,24,16,32,1]{1,2,4,3,0:T(8,128)(2,1)}, u32[]{:S(2)}) copy-start(bf16[1,24,16,32,1]{1,2,4,3,0:T(8,128)(2,1)} %copy.628) | copy-start | bytes 73732
  88.7 11.9 %copy-start.6 = (bf16[1,24,16,32,1]{1,2,4,3,0:T(8,128)(2,1)S(1)}, bf16[1,24,16,32,1]{1,2,4,3,0:T(8,128)(2,1)}, u32[]{:S(2)}) copy-start(bf16[1,24,16,32,1]{1,2,4,3,0:T(8,128)(2,1)} %copy.626) | copy-start | bytes 73732
  254.0 9.9 %copy-start.10 = (pred[48,4]{0,1:T(4,128)(4,1)S(1)}, pred[48,4]{0,1:T(4,128)(4,1)}, u32[]{:S(2)}) copy-start(pred[48,4]{0,1:T(4,128)(4,1)} %slice_compare_fusion) | copy-start | bytes 580
  263.8 8.8 %slice-start = ((s8[6684672]{0:T(1024)(128)(4,1)}), s8[4194304]{0:T(1024)(128)(4,1)S(1)}, s32[]{:S(2)}) async-start(s8[6684672]{0:T(1024)(128)(4,1)} %bitcast.210), calls=%async_computation | async-start | bytes 8388608
  264.9 7.7 %slice-start.1 = ((s8[6684672]{0:T(1024)(128)(4,1)}), s8[2490368]{0:T(1024)(128)(4,1)S(1)}, s32[]{:S(2)}) async-start(s8[6684672]{0:T(1024)(128)(4,1)} %bitcast.210), calls=%async_computation.1 | async-start | bytes 4980736
  276.0 9.8 %copy-start.8 = (pred[24,4]{1,0:T(8,128)(4,1)S(1)}, pred[24,4]{1,0:T(8,128)(4,1)}, u32[]{:S(2)}) copy-start(pred[24,4]{1,0:T(8,128)(4,1)} %copy.637) | copy-start | bytes 292
  276.0 21.7 %copy-start.7 = (pred[24,48,8]{1,0,2:T(8,128)(4,1)S(1)}, pred[24,48,8]{1,0,2:T(8,128)(4,1)}, u32[]{:S(2)}) copy-start(pred[24,48,8]{1,0,2:T(8,128)(4,1)} %broadcast_compare_fusion) | copy-start | bytes 27652
  276.0 21.7 %copy-start.9 = (pred[4,48,8]{1,2,0:T(8,128)(4,1)S(1)}, pred[4,48,8]{1,2,0:T(8,128)(4,1)}, u32[]{:S(2)}) copy-start(pred[4,48,8]{1,2,0:T(8,128)(4,1)} %iota_compare_fusion.4) | copy-start | bytes 4612
  284.3 13.4 %copy-start.4 = (f32[1,48,4,16,32]{1,3,2,4,0:T(8,128)S(1)}, f32[1,48,4,16,32]{1,3,2,4,0:T(8,128)}, u32[]{:S(2)}) copy-start(f32[1,48,4,16,32]{1,3,2,4,0:T(8,128)} %reverse_select_fusion) | copy-start | bytes 1179652
where the time goes:
time: 437 us; the launch traced here: 428 us
  local copies, waits for them, and re-layouts  191 us (44%)
  matrix products  129 us (30%)
  blocking collectives  69.5 us (16%)
  other arithmetic  37.4 us (9%)
    scatter-add x1, local copies, waits for them, and re-layouts, body(): inner = inner.at[..., -1, :].add(arrived[:, :, 1])  62.8 us
    conv_general_dilated x1, matrix products, body(): lax.conv_general_dilated(cot_flat, turned, (1, 1), ((2, 2), (2, 2)), dime...  61.8 us
    dot_general x9, matrix products, body(): jnp.einsum('nihw,nohw->oi', stacked_tiles[:, :, row_tap:row_tap + tile_si...  48.5 us
    psum x1, blocking collectives, body(): lax.psum((kernel_sum * factor, bias_sum * factor), ('dp', 'tile'))  42.1 us
    conv_general_dilated x1, matrix products, body(): lax.conv_general_dilated(stacked_tiles, weights, (1, 1), 'VALID', dimensi...  15 us
    scatter-add x1, local copies, waits for them, and re-layouts, body(): inner = inner.at[..., 0, :].add(arrived[:, :, 0])  14.7 us
    another operation x3, local copies, waits for them, and re-layouts  13.5 us
    unnamed x30, local copies, waits for them, and re-layouts  13 us

commit v1 on v0

v1 whole, which is shorter than its diff:
```python
import math

import jax
import jax.numpy as jnp
import numpy as np
from jax import lax
from jax.experimental import pallas as pl
from jax.experimental.pallas import tpu as pltpu
from jax.sharding import PartitionSpec as P

TS = 32


edge_table = np.array(
    [
        [1, 2, 0, 3],
        [0, 3, 1, 2],
        [3, 1, 2, 0],
        [2, 0, 3, 1],
        [1, 1, 0, 0],
        [1, 0, 0, 1],
        [0, 1, 1, 0],
        [0, 0, 1, 1],
    ],
    dtype=np.int32,
)
flip_table = np.array(
    [
        [0, 0, 1, 1],
        [0, 0, 1, 1],
        [0, 1, 1, 0],
        [0, 1, 1, 0],
        [1, 0, 0, 1],
        [0, 0, 1, 1],
        [1, 1, 0, 0],
        [0, 1, 1, 0],
    ],
    dtype=np.int32,
)


def slot_tables(tile_map, neighbours, rotations):
    total_slots = tile_map.shape[0]
    places = jnp.arange(total_slots, dtype=jnp.int32)
    onehot = (tile_map[:, None] == places[None, :]).astype(jnp.int32)
    inverse = jnp.sum(
        (tile_map[None, :] == places[:, None]).astype(jnp.int32) * places[None, :], axis=1
    )
    tile_nbr = jnp.sum(onehot[:, :, None] * neighbours[None], axis=1)
    tile_rot = jnp.sum(onehot[:, :, None] * rotations[None], axis=1)
    slot_nbr = jnp.sum(
        (tile_nbr[:, :, None] == places[None, None, :]).astype(jnp.int32) * inverse[None, None, :],
        axis=2,
    )
    matches = (tile_rot[:, :, None] == jnp.arange(4, dtype=jnp.int32)).astype(jnp.int32)
    edge_code = jnp.sum(matches * jnp.asarray(edge_table)[None], axis=-1)
    flip_code = jnp.sum(matches * jnp.asarray(flip_table)[None], axis=-1)
    return (slot_nbr, edge_code, flip_code)


CELLS = TS * TS
LANES = 128
VMEM_LIMIT = 50 * 1024 * 1024


def column_picker():
    m = np.zeros((CELLS, LANES), np.float32)
    for h in range(TS):
        m[h * TS, 2 * TS + h] = 1
        m[h * TS + TS - 1, 3 * TS + h] = 1
    return m


def strip_variants():
    m = np.zeros((LANES, 8 * LANES), np.float32)
    for edge in range(4):
        for flip in range(2):
            for rep in range(4):
                for t in range(TS):
                    at = TS - 1 - t if flip else t
                    m[edge * TS + at, (edge * 2 + flip) * LANES + rep * TS + t] = 1
    return m


def rim_images():
    m = np.zeros((2 * LANES, CELLS + 3 * LANES), np.float32)
    for h in range(TS):
        m[2 * TS + h, h * TS] = 1
        m[3 * TS + h, h * TS + TS - 1] = 1
    tops = [LANES] + list(range(TS)) + [LANES + TS]
    lows = [LANES + 2 * TS] + list(range(TS, 2 * TS)) + [LANES + 3 * TS]
    for col_tap in range(3):
        for w in range(TS):
            m[tops[w + col_tap], CELLS + col_tap * LANES + w] = 1
            m[lows[w + col_tap], CELLS + col_tap * LANES + 3 * TS + w] = 1
    return m


def edge_images():
    m = np.zeros((LANES, CELLS), np.float32)
    for t in range(TS):
        m[t, t] = 1
        m[TS + t, (TS - 1) * TS + t] = 1
        m[2 * TS + t, t * TS] = 1
        m[3 * TS + t, t * TS + TS - 1] = 1
    return np.concatenate([m, m], axis=0)


def const(m):
    return jnp.asarray(m.astype(jnp.bfloat16))


def dot(a, b):
    return jnp.dot(a, b, preferred_element_type=jnp.float32)


def lane_ids(width):
    return lax.broadcasted_iota(jnp.int32, (16, width), 1)


def edges_kernel(x_ref, pick_ref, q_ref):
    n = x_ref.shape[0]
    x = x_ref[...].reshape(n * 16, CELLS)
    cols = dot(x, pick_ref[...])
    first = x[:, :LANES].astype(jnp.float32)
    last = pltpu.roll(x[:, CELLS - LANES :].astype(jnp.float32), 2 * TS, 1)
    lane = lax.broadcasted_iota(jnp.int32, (n * 16, LANES), 1)
    q = jnp.where(lane < TS, first, jnp.where(lane < 2 * TS, last, cols))
    q_ref[...] = q.astype(jnp.bfloat16).reshape(n, 16, LANES)


def back_kernel(g_ref, wt_ref, pick_ref, inner_ref, p_ref):
    lane = lane_ids(CELLS)
    w = lane % TS
    blk = lane_ids(LANES)
    for t in range(g_ref.shape[0]):
        z = dot(wt_ref[...], g_ref[t])
        rows, rim = [], []
        for a in range(3):
            z0, z1, z2 = (z[(a * 3 + c) * 16 : (a * 3 + c + 1) * 16] for c in range(3))
            rows.append(
                z1
                + jnp.where(w != TS - 1, pltpu.roll(z0, CELLS - 1, 1), 0.0)
                + jnp.where(w != 0, pltpu.roll(z2, 1, 1), 0.0)
            )
            rim.append(jnp.where(w == 0, z0, jnp.where(w == TS - 1, z2, 0.0)))

        def rows_added(y):
            up = jnp.where(lane < CELLS - TS, pltpu.roll(y[0], CELLS - TS, 1), 0.0)
            down = jnp.where(lane >= TS, pltpu.roll(y[2], TS, 1), 0.0)
            return y[1] + up + down

        inner_ref[t] = rows_added(rows)
        cols = dot(rows_added(rim).astype(jnp.bfloat16), pick_ref[...])
        first = rows[0][:, :LANES]
        last = pltpu.roll(rows[2][:, CELLS - LANES :], 2 * TS, 1)
        edge = jnp.where(blk < TS, first, jnp.where(blk < 2 * TS, last, cols))
        c0 = rim[0][:, :LANES]
        c2 = rim[2][:, CELLS - LANES :]
        corner = jnp.where(blk == 0, c0, 0.0)
        corner += jnp.where(blk == TS, pltpu.roll(c0, 1, 1), 0.0)
        corner += jnp.where(blk == 2 * TS, pltpu.roll(c2, LANES - TS, 1), 0.0)
        corner += jnp.where(blk == 3 * TS, pltpu.roll(c2, LANES - TS + 1, 1), 0.0)
        p_ref[t, :, :LANES] = edge.astype(jnp.bfloat16)
        p_ref[t, :, LANES:] = corner.astype(jnp.bfloat16)


def front_kernel(
    slots, fsrc_ref, q_ref, var_ref, img_ref, x_ref, g_ref, w_ref, bias_ref,
    out_ref, dw_ref, v_ref, rim_ref, ri_ref, col_ref,
):
    step = pl.program_id(0)
    blk = lane_ids(LANES)

    @pl.when(step == 0)
    def _():
        total = q_ref.shape[0]
        q = q_ref[...].reshape(total * 16, LANES)
        for j in range(8):
            got = dot(q, var_ref[:, j * LANES : (j + 1) * LANES])
            v_ref[j * total : (j + 1) * total] = got.reshape(total, 16, LANES)
        for s in range(slots):
            for half in range(2):
                parts = [v_ref[fsrc_ref[s * 8 + half * 4 + k]] for k in range(4)]
                rim = jnp.where(
                    blk < 2 * TS,
                    jnp.where(blk < TS, parts[0], parts[1]),
                    jnp.where(blk < 3 * TS, parts[2], parts[3]),
                )
                rim_ref[s, :, half * LANES : (half + 1) * LANES] = rim.astype(jnp.bfloat16)
        ri = dot(rim_ref[...].reshape(slots * 16, 2 * LANES), img_ref[...])
        ri_ref[...] = ri.reshape(slots, 16, CELLS + 3 * LANES)
        dw_ref[...] = jnp.zeros_like(dw_ref)
        for t in range(col_ref.shape[0]):
            col_ref[t, 144:160, :] = jnp.ones((16, CELLS), jnp.bfloat16)

    w = lane_ids(CELLS) % TS
    tiles = x_ref.shape[0]
    total = jnp.zeros(dw_ref.shape, jnp.float32)
    for t in range(tiles):
        s = step * tiles + t
        x = x_ref[t].astype(jnp.float32)
        lr = ri_ref[s, :, :CELLS]
        mids = [
            jnp.where(w == 0, lr, pltpu.roll(x, 1, 1)),
            x,
            jnp.where(w == TS - 1, lr, pltpu.roll(x, CELLS - 1, 1)),
        ]
        for c in range(3):
            rim = ri_ref[s, :, CELLS + c * LANES : CELLS + (c + 1) * LANES]
            down = pltpu.roll(mids[c], TS, 1)
            up = pltpu.roll(mids[c], CELLS - TS, 1)
            down = jnp.concatenate(
                [jnp.where(blk < TS, rim, down[:, :LANES]), down[:, LANES:]], axis=1
            )
            up = jnp.concatenate(
                [up[:, : CELLS - LANES], jnp.where(blk >= 3 * TS, rim, up[:, CELLS - LANES :])],
                axis=1,
            )
            for a, tap in enumerate((down, mids[c], up)):
                row = (a * 3 + c) * 16
                col_ref[t, row : row + 16, :] = tap.astype(jnp.bfloat16)
        col = col_ref[t]
        out_ref[t] = (dot(w_ref[...], col[:144]) + bias_ref[...]).astype(jnp.bfloat16)
        total += lax.dot_general(
            g_ref[t], col, (((1,), (1,)), ((), ())), preferred_element_type=jnp.float32
        )
    dw_ref[...] += total


def finish_kernel(slots, bsrc_ref, bdst_ref, p_ref, var_ref, img_ref, inner_ref, out_ref, u_ref, acc_ref, r_ref):
    total = p_ref.shape[0]
    blk = lane_ids(LANES)
    for kind in range(2):
        p = p_ref[:, :, kind * LANES : (kind + 1) * LANES].reshape(total * 16, LANES)
        for j in range(8):
            got = dot(p, var_ref[:, j * LANES : (j + 1) * LANES])
            at = (kind * 8 + j) * total
            u_ref[at : at + total] = got.reshape(total, 16, LANES)
    acc_ref[...] = jnp.zeros_like(acc_ref)

    def add(q, carry):
        for k in range(8):
            d = bdst_ref[q * 8 + k]
            acc_ref[d] = acc_ref[d] + u_ref[bsrc_ref[q * 8 + k]]
        return carry

    lax.fori_loop(0, total, add, 0)
    for s in range(slots):
        parts = [acc_ref[s * 4 + k] for k in range(4)]
        r = jnp.where(
            blk < 2 * TS,
            jnp.where(blk < TS, parts[0], parts[1]),
            jnp.where(blk < 3 * TS, parts[2], parts[3]),
        )
        hi = r.astype(jnp.bfloat16)
        r_ref[s, :, :LANES] = hi
        r_ref[s, :, LANES:] = (r - hi.astype(jnp.float32)).astype(jnp.bfloat16)
    add_in = dot(r_ref[...].reshape(slots * 16, 2 * LANES), img_ref[...])
    out = inner_ref[...].reshape(slots * 16, CELLS) + add_in
    out_ref[...] = out.astype(jnp.bfloat16).reshape(slots, 16, CELLS)


def params():
    return pltpu.CompilerParams(vmem_limit_bytes=VMEM_LIMIT)


def cost(flops, bytes_accessed):
    return pl.CostEstimate(flops=flops, bytes_accessed=bytes_accessed, transcendentals=0)


def body(fields, weights, bias, cotangent, neighbours, rotations, tile_map):
    batch_loc, slots, in_chans, cells = fields.shape
    out_chans = weights.shape[0]
    x = fields.reshape(slots, in_chans, cells)
    g = cotangent.reshape(slots, out_chans, cells)
    tiles = 3
    steps = slots // tiles
    f32, bf16 = jnp.float32, jnp.bfloat16
    pick = const(column_picker())
    variants = const(strip_variants())
    vmem = pl.BlockSpec(memory_space=pltpu.VMEM)
    smem = pl.BlockSpec(memory_space=pltpu.SMEM)

    def whole(*dims):
        return pl.BlockSpec(dims, lambda i, *_: (0,) * len(dims))

    def block(*dims):
        return pl.BlockSpec((tiles, *dims), lambda i, *_: (i,) + (0,) * len(dims))

    edges = pl.pallas_call(
        edges_kernel,
        out_shape=jax.ShapeDtypeStruct((slots, in_chans, LANES), bf16),
        in_specs=[vmem, vmem],
        out_specs=vmem,
        compiler_params=params(),
        cost_estimate=cost(slots * 16 * CELLS * 256, slots * 16 * CELLS * 2),
        name="edges",
    )(x, pick)
    all_edges = lax.all_gather(edges, "tile", axis=0, tiled=True)
    total = all_edges.shape[0]

    wt = weights.transpose(2, 3, 1, 0).reshape(9 * in_chans, out_chans)
    inner, rim_cot = pl.pallas_call(
        back_kernel,
        grid=(steps,),
        out_shape=(
            jax.ShapeDtypeStruct((slots, in_chans, cells), f32),
            jax.ShapeDtypeStruct((slots, in_chans, 2 * LANES), bf16),
        ),
        in_specs=[block(out_chans, cells), whole(*wt.shape), whole(*pick.shape)],
        out_specs=(block(in_chans, cells), block(in_chans, 2 * LANES)),
        compiler_params=params(),
        cost_estimate=cost(slots * 1024 * 144 * 128 * 8, slots * 64 * CELLS * 4),
        name="back",
    )(g, wt, pick)
    all_rims = lax.all_gather(rim_cot, "tile", axis=0, tiled=True)

    slot_nbr, edge_code, flip_code = slot_tables(tile_map, neighbours, rotations)
    base = lax.axis_index("tile") * slots
    src = (edge_code * 2 + flip_code) * total + slot_nbr
    fsrc = lax.dynamic_slice_in_dim(src, base, slots, 0).reshape(-1)
    here = slot_nbr - base
    bdst = jnp.where((here >= 0) & (here < slots), here * 4 + edge_code, slots * 4).reshape(-1)
    ks = jnp.arange(8, dtype=jnp.int32)[None, :]
    bsrc = ((ks * 2 + flip_code) * total + jnp.arange(total, dtype=jnp.int32)[:, None]).reshape(-1)

    wf = weights.transpose(0, 2, 3, 1).reshape(out_chans, 9 * in_chans)
    images = const(rim_images())
    outputs, sums = pl.pallas_call(
        lambda *refs: front_kernel(slots, *refs),
        grid_spec=pltpu.PrefetchScalarGridSpec(
            num_scalar_prefetch=1,
            grid=(steps,),
            in_specs=[
                whole(*all_edges.shape),
                whole(*variants.shape),
                whole(*images.shape),
                block(in_chans, cells),
                block(out_chans, cells),
                whole(*wf.shape),
                whole(out_chans, 1),
            ],
            out_specs=(block(out_chans, cells), whole(out_chans, 160)),
            scratch_shapes=[
                pltpu.VMEM((8 * total, in_chans, LANES), f32),
                pltpu.VMEM((slots, in_chans, 2 * LANES), bf16),
                pltpu.VMEM((slots, in_chans, CELLS + 3 * LANES), f32),
                pltpu.VMEM((tiles, 160, CELLS), bf16),
            ],
        ),
        out_shape=(
            jax.ShapeDtypeStruct((slots, out_chans, cells), bf16),
            jax.ShapeDtypeStruct((out_chans, 160), f32),
        ),
        compiler_params=params(),
        cost_estimate=cost(slots * 1024 * 144 * 256 * 8, slots * 64 * CELLS * 4),
        name="front",
    )(fsrc, all_edges, variants, images, x, g, wf, bias[:, None])
    factor = 1.0 / math.sqrt(
        batch_loc * lax.axis_size("dp") * slots * lax.axis_size("tile") * cells
    )
    sums = lax.psum(sums, ("dp", "tile")) * factor
    grad_weights = sums[:, :144].reshape(out_chans, 3, 3, in_chans).transpose(0, 3, 1, 2)
    grad_bias = sums[:, 144]

    edge_img = const(edge_images())
    grad_fields = pl.pallas_call(
        lambda *refs: finish_kernel(slots, *refs),
        out_shape=jax.ShapeDtypeStruct((slots, in_chans, cells), bf16),
        in_specs=[smem, smem, vmem, vmem, vmem, vmem],
        out_specs=vmem,
        scratch_shapes=[
            pltpu.VMEM((16 * total, in_chans, LANES), f32),
            pltpu.VMEM((4 * slots + 8, in_chans, LANES), f32),
            pltpu.VMEM((slots, in_chans, 2 * LANES), bf16),
        ],
        compiler_params=params(),
        cost_estimate=cost(slots * 1024 * 144 * 128 * 8, slots * 64 * CELLS * 4),
        name="finish",
    )(bsrc, bdst, all_rims, variants, edge_img, inner)
    return (
        outputs.reshape(cotangent.shape),
        grad_fields.reshape(fields.shape),
        grad_weights,
        grad_bias,
    )


def solution(mesh):
    placed = (P("dp", "tile", None, None), P(), P(), P("dp", "tile", None, None), P(), P(), P())
    return jax.shard_map(
        body,
        mesh=mesh,
        in_specs=placed,
        out_specs=(P("dp", "tile", None, None), P("dp", "tile", None, None), P(), P()),
        check_vma=False,
    )
```

time: 437 us -> 94.2 us (0.22); the launches traced: 428 us -> 93.6 us
  local copies, waits for them, and re-layouts: 191 us -> 7.55 us
  matrix products: 129 us -> 0 us
  other arithmetic: 37.4 us -> 5.72 us
  Pallas kernels: 0 us -> 25.7 us
  blocking collectives: 69.5 us -> 53.9 us
    scatter-add x2 -> x0, local copies, waits for them, and re-layouts: 77.5 us -> none  [the longest x1 62.8 us: body(): inner = inner.at[..., -1, :].add(arrived[:, :, 1])]
    conv_general_dilated x2 -> x0, matrix products: 76.9 us -> none  [the longest x1 61.8 us: body(): lax.conv_general_dilated(cot_flat, turned, (1, 1), ((2, 2), (2, 2)), dime...]
    dot_general x11 -> x0, matrix products: 52 us -> none  [the longest x9 48.5 us: body(): jnp.einsum('nihw,nohw->oi', stacked_tiles[:, :, row_tap:row_tap + tile_si...]
    another operation x16 -> x0, local copies, waits for them, and re-layouts: 26.8 us -> none
    pallas_call x0 -> x4, Pallas kernels: none -> 25.7 us  [the longest x1 10.7 us: body(): pl.pallas_call(lambda *refs: front_kernel(slots, *refs), grid_spec=pltpu....]
    slice x13 -> x2, local copies, waits for them, and re-layouts: 27 us -> 1.43 us  [the longest x1 0.73 us: body(): sums[:, :144].reshape(out_chans, 3, 3, in_chans).transpose(0, 3, 1, 2)]
    reshape x3 -> x2, local copies, waits for them, and re-layouts: 15.8 us -> 0.95 us  [the longest x1 0.85 us: body(): wf = weights.transpose(0, 2, 3, 1).reshape(out_chans, 9 * in_chans)]
    all_gather x3 -> x2, blocking collectives: 27.4 us -> 13.2 us  [the longest x1 6.76 us: body(): all_rims = lax.all_gather(rim_cot, 'tile', axis=0, tiled=True)]
where the time goes in v1:
time: 94.2 us; the launch traced here: 93.6 us
  blocking collectives  53.9 us (57%)
  Pallas kernels  25.7 us (27%)
  local copies, waits for them, and re-layouts  7.55 us (8%)
  other arithmetic  5.72 us (6%)
    psum x1, blocking collectives, body(): sums = lax.psum(sums, ('dp', 'tile')) * factor  40.8 us
    pallas_call x1, Pallas kernels, body(): pl.pallas_call(lambda *refs: front_kernel(slots, *refs), grid_spec=pltpu....  10.7 us
    pallas_call x1, Pallas kernels, body(): pl.pallas_call(back_kernel, grid=(steps,), out_shape=(jax.ShapeDtypeStruc...  9.96 us
    all_gather x1, blocking collectives, body(): all_rims = lax.all_gather(rim_cot, 'tile', axis=0, tiled=True)  6.76 us
    all_gather x1, blocking collectives, body(): all_edges = lax.all_gather(edges, 'tile', axis=0, tiled=True)  6.39 us
    pallas_call x1, Pallas kernels, body(): pl.pallas_call(lambda *refs: finish_kernel(slots, *refs), out_shape=jax.S...  4.63 us
    unnamed x16, local copies, waits for them, and re-layouts  3.81 us
    reduce_sum x1, other arithmetic, slot_tables(): tile_rot = jnp.sum(onehot[:, :, None] * rotations[None], axis=1)  2.4 us

profile of v1, /device:TPU:0, one launch (start us, length us, event | category | flops | bytes accessed | tf_op | source)
XLA Modules:
  0.0 93.6 jit_solution(15340574822019648119)
XLA Ops:
  0.6 0.8 select_reduce_fusion.1
  1.4 0.7 fusion
  2.1 2.4 %multiply_reduce_fusion.1 = (s32[48,8]{1,0:T(8,128)S(1)}, s32[48,8]{1,0:T(8,128)S(1)}) fusion(s32[48,8]{0,1:T(8,128)} %param.18, s32[48,48]{1,0:T(8,128)S(1)} %fusion, s32[48,8]{0,1:T(8,128)} %param.17), kind=kLoop, calls=%fused_computation.3 | loop fusion | flops 72960 | bytes 15360 | tf_op jit(solution)/shard_map/reduce_sum | solution.py:50
  4.5 0.1 copy.32
  4.6 0.8 select_reduce_fusion.3
  5.4 1.0 %select_reduce_fusion = s32[48,8]{1,0:T(8,128)S(1)} fusion(s32[48]{0:T(128)S(1)} %select_reduce_fusion.1, s32[48,8]{1,0:T(8,128)S(1)} %get-tuple-element.13), kind=kLoop, calls=%fused_computation | loop fusion | flops 54912 | bytes 3264 | tf_op jit(solution)/shard_map/reduce_sum | solution.py:51
  6.4 0.1 copy.33
  6.4 0.1 add_select_fusion
  6.5 0.1 constant_dynamic-slice_fusion
  6.6 0.1 copy.34
  6.6 0.1 reshape.90.refs_0_
  6.7 0.1 copy.39
  6.8 0.1 select_n.13.refs_1_
  6.9 0.1 copy.37
  7.0 0.1 add.45.refs_0_
  7.1 0.7 copy.36.refs_7_
  7.8 0.8 copy.35.refs_6_
  8.7 0.0 copy-start
  8.7 1.1 %copy-done = bf16[1,24,16,1024]{3,2,1,0:T(8,128)(2,1)S(1)} copy-done((bf16[1,24,16,1024]{3,2,1,0:T(8,128)(2,1)S(1)}, bf16[1,24,16,1024]{3,2,1,0:T(8,128)(2,1)}, u32[]{:S(2)}) %copy-start) | copy-done | bytes 786456
  9.8 0.9 %copy-done.2 = bf16[1024,128]{1,0:T(8,128)(2,1)S(1)} copy-done((bf16[1024,128]{1,0:T(8,128)(2,1)S(1)}, bf16[1024,128]{1,0:T(8,128)(2,1)}, u32[]{:S(2)}) %copy-start.2) | copy-done | bytes 262168
  10.8 0.4 edges.1
  11.2 6.4 %all_gather.6.refs_1_ = bf16[48,16,128]{2,1,0:T(8,128)(2,1)S(1)} all-gather(bf16[24,16,128]{2,1,0:T(8,128)(2,1)S(1)} %edges.1), channel_id=1, replica_groups=mesh['dp'=16,'tile'=2] {'tile'}, dimensions={0}, use_global_device_ids=true | all-gather | bytes 294912 | tf_op jit(solution)/shard_map/all_gather | solution.py:300
  17.6 0.9 %copy-done.3 = bf16[1024,128]{1,0:T(8,128)(2,1)S(1)} copy-done((bf16[1024,128]{1,0:T(8,128)(2,1)S(1)}, bf16[1024,128]{1,0:T(8,128)(2,1)}, u32[]{:S(2)}) %copy-start.3) | copy-done | bytes 262168
  18.5 0.8 copy-done.4
  19.3 10.0 %back.1 = (f32[24,16,1024]{2,1,0:T(8,128)S(1)}, bf16[24,16,256]{2,1,0:T(8,128)(2,1)S(1)}) custom-call(bf16[24,64,1024]{2,1,0:T(8,128)(2,1)} %bitcast.22, bf16[144,64]{1,0:T(8,128)(2,1)S(1)} %bitcast.18, bf16[1024,128]{1,0:T(8,128)(2,1)S(1)} %copy-done.3), custom_call_target="tpu_custom_call" | custom-call | flops 3623878656 | bytes 6291456 | tf_op jit(solution)/shard_map/back/pallas_call | solution.py:304
  29.2 6.8 %all_gather.7.refs_2_ = bf16[48,16,256]{2,1,0:T(8,128)(2,1)S(1)} all-gather(bf16[24,16,256]{2,1,0:T(8,128)(2,1)S(1)} %get-tuple-element.9), channel_id=1, replica_groups=mesh['dp'=16,'tile'=2] {'tile'}, dimensions={0}, use_global_device_ids=true | all-gather | bytes 589824 | tf_op jit(solution)/shard_map/all_gather | solution.py:317
  36.0 0.0 copy-done.6
  36.0 4.6 %finish.1 = bf16[24,16,1024]{2,1,0:T(8,128)(2,1)} custom-call(s32[384]{0:T(512)S(1)} %add.45.refs_0_, s32[384]{0:T(512)S(1)} %select_n.13.refs_1_, bf16[48,16,256]{2,1,0:T(8,128)(2,1)S(1)} %all_gather.7.refs_2_, bf16[128,1024]{1,0:T(8,128)(2,1)S(1)} %copy-done.7, bf16[256,1024]{1,0:T(8,128)(2,1)S(1)} %copy-done.6, f32[24,16,1024]{2,1,0:T(8,128)S(1)} %get-tuple-element.10.refs_5_), custom_call_target="tpu_custom_call" | custom-call | flops 3623878656 | bytes 6291456 | tf_op jit(solution)/shard_map/finish/pallas_call | solution.py:368
  40.7 10.7 %front.1 = (bf16[24,64,1024]{2,1,0:T(8,128)(2,1)}, f32[64,160]{1,0:T(8,128)S(1)}) custom-call(s32[192]{0:T(256)S(1)} %reshape.90.refs_0_, bf16[48,16,128]{2,1,0:T(8,128)(2,1)S(1)} %all_gather.6.refs_1_, bf16[128,1024]{1,0:T(8,128)(2,1)S(1)} %copy-done.7, bf16[256,1408]{1,0:T(8,128)(2,1)S(1)} %copy-done.5, bf16[24,16,1024]{2,1,0:T(8,128)(2,1)S(1)} %bitcast.16, ...), custom_call_target="tpu_custom_call" | custom-call | flops 7247757312 | bytes 6291456 | tf_op jit(solution)/shard_map/front/pallas_call | solution.py:330
  51.4 40.8 %psum.7 = f32[64,160]{1,0:T(8,128)S(1)} all-reduce(f32[64,160]{1,0:T(8,128)S(1)} %get-tuple-element.11), channel_id=1, replica_groups=mesh['dp'=16,'tile'=2] {'dp','tile'}, use_global_device_ids=true, to_apply=%region_6.7 | all-reduce | flops 10240 | bytes 81920 | tf_op jit(solution)/shard_map/psum | solution.py:363
  92.1 0.7 slice_reduce_fusion
  92.8 0.7 copy.40
  (12 shorter events, 0.0 us)
Async XLA Ops:
  8.7 1.1 %copy-start = (bf16[1,24,16,1024]{3,2,1,0:T(8,128)(2,1)S(1)}, bf16[1,24,16,1024]{3,2,1,0:T(8,128)(2,1)}, u32[]{:S(2)}) copy-start(bf16[1,24,16,1024]{3,2,1,0:T(8,128)(2,1)} %param.13) | copy-start | bytes 2359300
  9.8 0.9 %copy-start.2 = (bf16[1024,128]{1,0:T(8,128)(2,1)S(1)}, bf16[1024,128]{1,0:T(8,128)(2,1)}, u32[]{:S(2)}) copy-start(bf16[1024,128]{1,0:T(8,128)(2,1)} %constant.38.clone.pick_ref) | copy-start | bytes 786436
  17.5 1.0 %copy-start.3 = (bf16[1024,128]{1,0:T(8,128)(2,1)S(1)}, bf16[1024,128]{1,0:T(8,128)(2,1)}, u32[]{:S(2)}) copy-start(bf16[1024,128]{1,0:T(8,128)(2,1)} %constant.38.clone.pick_ref) | copy-start | bytes 786436
  18.5 0.8 copy-start.4
  19.3 16.7 %copy-start.6 = (bf16[256,1024]{1,0:T(8,128)(2,1)S(1)}, bf16[256,1024]{1,0:T(8,128)(2,1)}, u32[]{:S(2)}) copy-start(bf16[256,1024]{1,0:T(8,128)(2,1)} %constant.43.clone.refs_4_) | copy-start | bytes 1572868
  19.3 16.7 %copy-start.7 = (bf16[128,1024]{1,0:T(8,128)(2,1)S(1)}, bf16[128,1024]{1,0:T(8,128)(2,1)}, u32[]{:S(2)}) copy-start(bf16[128,1024]{1,0:T(8,128)(2,1)} %constant.39.clone.refs_2_.refs_3_) | copy-start | bytes 786436
  36.0 4.6 %copy-start.1 = (bf16[1,24,16,1024]{3,2,1,0:T(8,128)(2,1)S(1)}, bf16[1,24,16,1024]{3,2,1,0:T(8,128)(2,1)}, u32[]{:S(2)}) copy-start(bf16[1,24,16,1024]{3,2,1,0:T(8,128)(2,1)} %param.13) | copy-start | bytes 2359300
  36.0 4.6 %copy-start.5 = (bf16[256,1408]{1,0:T(8,128)(2,1)S(1)}, bf16[256,1408]{1,0:T(8,128)(2,1)}, u32[]{:S(2)}) copy-start(bf16[256,1408]{1,0:T(8,128)(2,1)} %constant.42.clone.refs_3_) | copy-start | bytes 2162692

commit v2 on v1

--- a/solution.py
+++ b/solution.py
@@ -259,6 +259,68 @@
     add_in = dot(r_ref[...].reshape(slots * 16, 2 * LANES), img_ref[...])
     out = inner_ref[...].reshape(slots * 16, CELLS) + add_in
     out_ref[...] = out.astype(jnp.bfloat16).reshape(slots, 16, CELLS)
+
+
+def sum_kernel(dp_size, tile_size, factor, in_ref, out_ref, near_ref, far_ref, near_send, near_recv, far_send, far_recv):
+    dp, tile = lax.axis_index("dp"), lax.axis_index("tile")
+    pairs = dp_size // 2
+    core, hi = lax.rem(dp, 2), dp // 2
+    near_count = 2 * tile_size
+
+    def near_peer(j):
+        return (hi * 2 + lax.rem(core + j % 2, 2), lax.rem(tile + j // 2, tile_size))
+
+    def far_peer(j):
+        return (lax.rem(hi + j, pairs) * 2 + core, tile)
+
+    peers = [near_peer(j) for j in range(1, near_count)] + [far_peer(j) for j in range(1, pairs)]
+    barrier = pltpu.get_barrier_semaphore()
+    for peer in peers:
+        pl.semaphore_signal(barrier, inc=1, device_id=peer, device_id_type=pl.DeviceIdType.MESH)
+
+    rows = in_ref.shape[0]
+    quarter = rows // 4
+    rest = in_ref[:, LANES:]
+    packed = jnp.concatenate(
+        [
+            in_ref[:, :LANES],
+            jnp.concatenate([rest[k * quarter : (k + 1) * quarter] for k in range(4)], axis=1),
+        ],
+        axis=0,
+    )
+    pl.semaphore_wait(barrier, len(peers))
+
+    def exchange(value, ref, me, count, peer_of, send, recv):
+        ref[me] = value
+        copies = []
+        for j in range(1, count):
+            copy = pltpu.make_async_remote_copy(
+                src_ref=ref.at[me],
+                dst_ref=ref.at[me],
+                send_sem=send.at[j],
+                recv_sem=recv.at[j],
+                device_id=peer_of(j),
+                device_id_type=pl.DeviceIdType.MESH,
+            )
+            copy.start()
+            copies.append(copy)
+        for copy in copies:
+            copy.wait_recv()
+        total = ref[0]
+        for j in range(1, count):
+            total = total + ref[j]
+        return total, copies
+
+    near, near_copies = exchange(
+        packed, near_ref, core * tile_size + tile, near_count, near_peer, near_send, near_recv
+    )
+    far, far_copies = exchange(near, far_ref, hi, pairs, far_peer, far_send, far_recv)
+    far = far * factor
+    out_ref[:, :LANES] = far[:rows]
+    for k in range(4):
+        out_ref[k * quarter : (k + 1) * quarter, LANES:] = far[rows:, k * 32 : (k + 1) * 32]
+    for copy in near_copies + far_copies:
+        copy.wait_send()
 
 
 def params():
@@ -360,7 +422,26 @@
     factor = 1.0 / math.sqrt(
         batch_loc * lax.axis_size("dp") * slots * lax.axis_size("tile") * cells
     )
-    sums = lax.psum(sums, ("dp", "tile")) * factor
+    dp_size, tile_size = lax.axis_size("dp"), lax.axis_size("tile")
+    packed_rows = out_chans + out_chans // 4
+    sums = pl.pallas_call(
+        lambda *refs: sum_kernel(dp_size, tile_size, factor, *refs),
+        out_shape=jax.ShapeDtypeStruct((out_chans, 160), f32),
+        in_specs=[vmem],
+        out_specs=vmem,
+        scratch_shapes=[
+            pltpu.VMEM((2 * tile_size, packed_rows, LANES), f32),
+            pltpu.VMEM((dp_size // 2, packed_rows, LANES), f32),
+            pltpu.SemaphoreType.DMA((2 * tile_size,)),
+            pltpu.SemaphoreType.DMA((2 * tile_size,)),
+            pltpu.SemaphoreType.DMA((dp_size // 2,)),
+            pltpu.SemaphoreType.DMA((dp_size // 2,)),
+        ],
+        compiler_params=pltpu.CompilerParams(
+            collective_id=0, has_side_effects=True, vmem_limit_bytes=VMEM_LIMIT
+        ),
+        name="sums",
+    )(sums)
     grad_weights = sums[:, :144].reshape(out_chans, 3, 3, in_chans).transpose(0, 3, 1, 2)
     grad_bias = sums[:, 144]
 

time: 94.2 us -> 68.2 us (0.72)
  blocking collectives: 53.9 us -> 13.2 us
  Pallas kernels: 25.7 us -> 40.4 us
    psum x1 -> x0, blocking collectives: 40.8 us -> none  [body(): sums = lax.psum(sums, ('dp', 'tile')) * factor]
    pallas_call x0 -> x1, Pallas kernels: none -> 14.7 us  [body(): pl.pallas_call(lambda *refs: sum_kernel(dp_size, tile_size, factor, *refs...]
where the time goes in v2:
time: 68.2 us; the launch traced here: 67.5 us
  Pallas kernels  40.4 us (59%)
  blocking collectives  13.2 us (19%)
  local copies, waits for them, and re-layouts  7.55 us (11%)
  other arithmetic  5.71 us (8%)
  between operations  0.72 us (1%)
    pallas_call x1, Pallas kernels, body(): pl.pallas_call(lambda *refs: sum_kernel(dp_size, tile_size, factor, *refs...  14.7 us
    pallas_call x1, Pallas kernels, body(): pl.pallas_call(lambda *refs: front_kernel(slots, *refs), grid_spec=pltpu....  10.7 us
    pallas_call x1, Pallas kernels, body(): pl.pallas_call(back_kernel, grid=(steps,), out_shape=(jax.ShapeDtypeStruc...  9.96 us
    all_gather x1, blocking collectives, body(): all_rims = lax.all_gather(rim_cot, 'tile', axis=0, tiled=True)  6.76 us
    all_gather x1, blocking collectives, body(): all_edges = lax.all_gather(edges, 'tile', axis=0, tiled=True)  6.39 us
    pallas_call x1, Pallas kernels, body(): pl.pallas_call(lambda *refs: finish_kernel(slots, *refs), out_shape=jax.S...  4.65 us
    unnamed x16, local copies, waits for them, and re-layouts  3.81 us
    reduce_sum x1, other arithmetic, slot_tables(): tile_rot = jnp.sum(onehot[:, :, None] * rotations[None], axis=1)  2.4 us

profile of v2, /device:TPU:0, one launch (start us, length us, event | category | flops | bytes accessed | tf_op | source)
XLA Modules:
  0.0 67.5 jit_solution(298512034368626516)
XLA Ops:
  0.6 0.8 %select_reduce_fusion.1 = s32[48]{0:T(128)S(1)} fusion(s32[48]{0:T(128)} %param.19), kind=kLoop, calls=%fused_computation.5 | loop fusion | flops 6864 | bytes 384 | tf_op jit(solution)/shard_map/reduce_sum | solution.py:46
  1.4 0.7 %fusion = s32[48,48]{1,0:T(8,128)S(1)} fusion(s32[48]{0:T(128)} %param.19), kind=kLoop, calls=%fused_computation.8 | loop fusion | flops 4608 | bytes 9408 | tf_op jit(solution)/shard_map/convert_element_type | solution.py:45
  2.1 2.4 %multiply_reduce_fusion.1 = (s32[48,8]{1,0:T(8,128)S(1)}, s32[48,8]{1,0:T(8,128)S(1)}) fusion(s32[48,8]{0,1:T(8,128)} %param.18, s32[48,48]{1,0:T(8,128)S(1)} %fusion, s32[48,8]{0,1:T(8,128)} %param.17), kind=kLoop, calls=%fused_computation.3 | loop fusion | flops 72960 | bytes 15360 | tf_op jit(solution)/shard_map/reduce_sum | solution.py:50
  4.5 0.1 copy.32
  4.6 0.8 %select_reduce_fusion.3 = (s32[48,8]{0,1:T(8,128)S(1)}, s32[48,8]{0,1:T(8,128)S(1)}) fusion(s32[8,4]{0,1:T(4,128)} %constant.38.clone, s32[48,8]{0,1:T(8,128)S(1)} %copy.32, s32[8,4]{0,1:T(4,128)} %constant.39.clone), kind=kLoop, calls=%fused_computation.10 | loop fusion | flops 6912 | bytes 4864 | tf_op jit(solution)/shard_map/reduce_sum | solution.py:56
  5.4 1.0 %select_reduce_fusion = s32[48,8]{1,0:T(8,128)S(1)} fusion(s32[48]{0:T(128)S(1)} %select_reduce_fusion.1, s32[48,8]{1,0:T(8,128)S(1)} %get-tuple-element.13), kind=kLoop, calls=%fused_computation | loop fusion | flops 54912 | bytes 3264 | tf_op jit(solution)/shard_map/reduce_sum | solution.py:51
  6.4 0.1 copy.33
  6.4 0.1 add_select_fusion
  6.5 0.1 constant_dynamic-slice_fusion
  6.6 0.1 copy.34
  6.6 0.1 reshape.90.refs_0_
  6.7 0.1 copy.39
  6.8 0.1 select_n.13.refs_1_
  6.9 0.1 copy.37
  7.0 0.1 add.43.refs_0_
  7.1 0.7 %copy.36.refs_7_ = f32[64,1]{1,0:T(8,128)S(1)} copy(f32[64,1]{0,1:T(1,128)} %bitcast.21) | data formatting | bytes 512 | tf_op jit(solution)/shard_map/broadcast_in_dim | solution.py:421
  7.8 0.8 %copy.35.refs_6_ = bf16[64,144]{1,0:T(8,128)(2,1)S(1)} copy(bf16[64,144]{0,1:T(8,128)(2,1)} %bitcast.18) | data formatting | bytes 36864 | tf_op jit(solution)/shard_map/reshape | solution.py:390
  8.7 0.0 copy-start
  8.7 1.1 %copy-done = bf16[1,24,16,1024]{3,2,1,0:T(8,128)(2,1)S(1)} copy-done((bf16[1,24,16,1024]{3,2,1,0:T(8,128)(2,1)S(1)}, bf16[1,24,16,1024]{3,2,1,0:T(8,128)(2,1)}, u32[]{:S(2)}) %copy-start) | copy-done | bytes 786456
  9.8 0.9 %copy-done.2 = bf16[1024,128]{1,0:T(8,128)(2,1)S(1)} copy-done((bf16[1024,128]{1,0:T(8,128)(2,1)S(1)}, bf16[1024,128]{1,0:T(8,128)(2,1)}, u32[]{:S(2)}) %copy-start.2) | copy-done | bytes 262168
  10.8 0.4 edges.1
  11.2 6.4 %all_gather.6.refs_1_ = bf16[48,16,128]{2,1,0:T(8,128)(2,1)S(1)} all-gather(bf16[24,16,128]{2,1,0:T(8,128)(2,1)S(1)} %edges.1), channel_id=1, replica_groups=mesh['dp'=16,'tile'=2] {'tile'}, dimensions={0}, use_global_device_ids=true | all-gather | bytes 294912 | tf_op jit(solution)/shard_map/all_gather | solution.py:362
  17.6 0.9 %copy-done.3 = bf16[1024,128]{1,0:T(8,128)(2,1)S(1)} copy-done((bf16[1024,128]{1,0:T(8,128)(2,1)S(1)}, bf16[1024,128]{1,0:T(8,128)(2,1)}, u32[]{:S(2)}) %copy-start.3) | copy-done | bytes 262168
  18.5 0.8 %copy-done.4 = bf16[64,16,3,3]{0,1,3,2:T(8,128)(2,1)S(1)} copy-done((bf16[64,16,3,3]{0,1,3,2:T(8,128)(2,1)S(1)}, bf16[64,16,3,3]{0,1,3,2:T(8,128)(2,1)}, u32[]{:S(2)}) %copy-start.4) | copy-done | bytes 18456
  19.3 10.0 %back.1 = (f32[24,16,1024]{2,1,0:T(8,128)S(1)}, bf16[24,16,256]{2,1,0:T(8,128)(2,1)S(1)}) custom-call(bf16[24,64,1024]{2,1,0:T(8,128)(2,1)} %bitcast.22, bf16[144,64]{1,0:T(8,128)(2,1)S(1)} %bitcast.19, bf16[1024,128]{1,0:T(8,128)(2,1)S(1)} %copy-done.3), custom_call_target="tpu_custom_call" | custom-call | flops 3623878656 | bytes 6291456 | tf_op jit(solution)/shard_map/back/pallas_call | solution.py:366
  29.2 6.8 %all_gather.7.refs_2_ = bf16[48,16,256]{2,1,0:T(8,128)(2,1)S(1)} all-gather(bf16[24,16,256]{2,1,0:T(8,128)(2,1)S(1)} %get-tuple-element.9), channel_id=1, replica_groups=mesh['dp'=16,'tile'=2] {'tile'}, dimensions={0}, use_global_device_ids=true | all-gather | bytes 589824 | tf_op jit(solution)/shard_map/all_gather | solution.py:379
  36.0 4.7 %finish.1 = bf16[24,16,1024]{2,1,0:T(8,128)(2,1)} custom-call(s32[384]{0:T(512)S(1)} %add.43.refs_0_, s32[384]{0:T(512)S(1)} %select_n.13.refs_1_, bf16[48,16,256]{2,1,0:T(8,128)(2,1)S(1)} %all_gather.7.refs_2_, bf16[128,1024]{1,0:T(8,128)(2,1)S(1)} %copy-done.7, bf16[256,1024]{1,0:T(8,128)(2,1)S(1)} %copy-done.6, f32[24,16,1024]{2,1,0:T(8,128)S(1)} %get-tuple-element.10.refs_5_), custom_call_target="tpu_custom_call" | custom-call | flops 3623878656 | bytes 6291456 | tf_op jit(solution)/shard_map/finish/pallas_call | solution.py:449
  40.7 0.0 copy-done.1
  40.7 10.7 %front.1 = (bf16[24,64,1024]{2,1,0:T(8,128)(2,1)}, f32[64,160]{1,0:T(8,128)S(1)}) custom-call(s32[192]{0:T(256)S(1)} %reshape.90.refs_0_, bf16[48,16,128]{2,1,0:T(8,128)(2,1)S(1)} %all_gather.6.refs_1_, bf16[128,1024]{1,0:T(8,128)(2,1)S(1)} %copy-done.7, bf16[256,1408]{1,0:T(8,128)(2,1)S(1)} %copy-done.5, bf16[24,16,1024]{2,1,0:T(8,128)(2,1)S(1)} %bitcast.16, ...), custom_call_target="tpu_custom_call" | custom-call | flops 7247757312 | bytes 6291456 | tf_op jit(solution)/shard_map/front/pallas_call | solution.py:392
  51.4 14.7 %sums.1 = f32[64,160]{1,0:T(8,128)S(1)} custom-call(f32[64,160]{1,0:T(8,128)S(1)} %get-tuple-element.11.refs_0_), custom_call_target="tpu_custom_call" | custom-call | tf_op jit(solution)/shard_map/sums/pallas_call | solution.py:427
  66.1 0.7 %slice_reduce_fusion = f32[64]{0:T(128)} fusion(f32[64,160]{1,0:T(8,128)S(1)} %sums.1), kind=kLoop, calls=%fused_computation.4 | loop fusion | bytes 512 | tf_op jit(solution)/shard_map/slice | solution.py:446
  66.8 0.7 %copy.40 = f32[64,144]{0,1:T(8,128)} copy(f32[64,144]{1,0:T(8,128)S(1)} %bitcast.17) | data formatting | bytes 73728 | tf_op jit(solution)/shard_map/slice | solution.py:445
  (11 shorter events, 0.0 us)
Async XLA Ops:
  8.7 1.1 %copy-start = (bf16[1,24,16,1024]{3,2,1,0:T(8,128)(2,1)S(1)}, bf16[1,24,16,1024]{3,2,1,0:T(8,128)(2,1)}, u32[]{:S(2)}) copy-start(bf16[1,24,16,1024]{3,2,1,0:T(8,128)(2,1)} %param.13) | copy-start | bytes 2359300
  9.8 0.9 %copy-start.2 = (bf16[1024,128]{1,0:T(8,128)(2,1)S(1)}, bf16[1024,128]{1,0:T(8,128)(2,1)}, u32[]{:S(2)}) copy-start(bf16[1024,128]{1,0:T(8,128)(2,1)} %constant.36.clone.pick_ref) | copy-start | bytes 786436
  17.5 1.0 %copy-start.3 = (bf16[1024,128]{1,0:T(8,128)(2,1)S(1)}, bf16[1024,128]{1,0:T(8,128)(2,1)}, u32[]{:S(2)}) copy-start(bf16[1024,128]{1,0:T(8,128)(2,1)} %constant.36.clone.pick_ref) | copy-start | bytes 786436
  18.5 0.8 %copy-start.4 = (bf16[64,16,3,3]{0,1,3,2:T(8,128)(2,1)S(1)}, bf16[64,16,3,3]{0,1,3,2:T(8,128)(2,1)}, u32[]{:S(2)}) copy-start(bf16[64,16,3,3]{0,1,3,2:T(8,128)(2,1)} %param.14) | copy-start | bytes 55300
  19.3 16.7 %copy-start.6 = (bf16[256,1024]{1,0:T(8,128)(2,1)S(1)}, bf16[256,1024]{1,0:T(8,128)(2,1)}, u32[]{:S(2)}) copy-start(bf16[256,1024]{1,0:T(8,128)(2,1)} %constant.41.clone.refs_4_) | copy-start | bytes 1572868
  19.3 16.7 %copy-start.7 = (bf16[128,1024]{1,0:T(8,128)(2,1)S(1)}, bf16[128,1024]{1,0:T(8,128)(2,1)}, u32[]{:S(2)}) copy-start(bf16[128,1024]{1,0:T(8,128)(2,1)} %constant.37.clone.refs_2_.refs_3_) | copy-start | bytes 786436
  36.0 4.7 %copy-start.1 = (bf16[1,24,16,1024]{3,2,1,0:T(8,128)(2,1)S(1)}, bf16[1,24,16,1024]{3,2,1,0:T(8,128)(2,1)}, u32[]{:S(2)}) copy-start(bf16[1,24,16,1024]{3,2,1,0:T(8,128)(2,1)} %param.13) | copy-start | bytes 2359300
  36.0 4.7 %copy-start.5 = (bf16[256,1408]{1,0:T(8,128)(2,1)S(1)}, bf16[256,1408]{1,0:T(8,128)(2,1)}, u32[]{:S(2)}) copy-start(bf16[256,1408]{1,0:T(8,128)(2,1)} %constant.40.clone.refs_3_) | copy-start | bytes 2162692

commit v3 on v2

--- a/solution.py
+++ b/solution.py
@@ -118,22 +118,58 @@
     return lax.broadcasted_iota(jnp.int32, (16, width), 1)
 
 
-def edges_kernel(x_ref, pick_ref, q_ref):
-    n = x_ref.shape[0]
-    x = x_ref[...].reshape(n * 16, CELLS)
-    cols = dot(x, pick_ref[...])
-    first = x[:, :LANES].astype(jnp.float32)
-    last = pltpu.roll(x[:, CELLS - LANES :].astype(jnp.float32), 2 * TS, 1)
-    lane = lax.broadcasted_iota(jnp.int32, (n * 16, LANES), 1)
-    q = jnp.where(lane < TS, first, jnp.where(lane < 2 * TS, last, cols))
-    q_ref[...] = q.astype(jnp.bfloat16).reshape(n, 16, LANES)
-
-
-def back_kernel(g_ref, wt_ref, pick_ref, inner_ref, p_ref):
+def gather_kernel(
+    tile_size, x_ref, g_ref, wt_ref, pick_ref, inner_ref, edges_ref, rims_ref,
+    q_all, p_all, q_send, q_recv, p_send, p_recv,
+):
+    step = pl.program_id(0)
+    slots, tiles = x_ref.shape[0], g_ref.shape[0]
+    steps = slots // tiles
+    dp, tile = lax.axis_index("dp"), lax.axis_index("tile")
+    base = tile * slots
+    barrier = pltpu.get_barrier_semaphore()
+    mesh_ids = pl.DeviceIdType.MESH
+
+    def peer(j):
+        return (dp, lax.rem(tile + j, tile_size))
+
+    def edges_copy(j):
+        part = q_all.at[pl.ds(base, slots)]
+        return pltpu.make_async_remote_copy(
+            src_ref=part, dst_ref=part, send_sem=q_send.at[j], recv_sem=q_recv.at[j],
+            device_id=peer(j), device_id_type=mesh_ids,
+        )
+
+    def rims_copy(j, i):
+        part = p_all.at[pl.ds(base + i * tiles, tiles)]
+        return pltpu.make_async_remote_copy(
+            src_ref=part, dst_ref=part, send_sem=p_send.at[j, i], recv_sem=p_recv.at[j, i],
+            device_id=peer(j), device_id_type=mesh_ids,
+        )
+
+    @pl.when(step == 0)
+    def _():
+        for j in range(1, tile_size):
+            pl.semaphore_signal(barrier, inc=1, device_id=peer(j), device_id_type=mesh_ids)
+        x = x_ref[...].reshape(slots * 16, CELLS)
+        cols = dot(x, pick_ref[...])
+        first = x[:, :LANES].astype(jnp.float32)
+        last = pltpu.roll(x[:, CELLS - LANES :].astype(jnp.float32), 2 * TS, 1)
+        lane = lax.broadcasted_iota(jnp.int32, (slots * 16, LANES), 1)
+        q = jnp.where(lane < TS, first, jnp.where(lane < 2 * TS, last, cols))
+        q_all[pl.ds(base, slots)] = q.astype(jnp.bfloat16).reshape(slots, 16, LANES)
+
     lane = lane_ids(CELLS)
     w = lane % TS
     blk = lane_ids(LANES)
-    for t in range(g_ref.shape[0]):
+
+    def rows_added(y):
+        up = jnp.where(lane < CELLS - TS, pltpu.roll(y[0], CELLS - TS, 1), 0.0)
+        down = jnp.where(lane >= TS, pltpu.roll(y[2], TS, 1), 0.0)
+        return y[1] + up + down
+
+    kept, sides = [], []
+    for t in range(tiles):
         z = dot(wt_ref[...], g_ref[t])
         rows, rim = [], []
         for a in range(3):
@@ -144,25 +180,43 @@
                 + jnp.where(w != 0, pltpu.roll(z2, 1, 1), 0.0)
             )
             rim.append(jnp.where(w == 0, z0, jnp.where(w == TS - 1, z2, 0.0)))
-
-        def rows_added(y):
-            up = jnp.where(lane < CELLS - TS, pltpu.roll(y[0], CELLS - TS, 1), 0.0)
-            down = jnp.where(lane >= TS, pltpu.roll(y[2], TS, 1), 0.0)
-            return y[1] + up + down
-
         inner_ref[t] = rows_added(rows)
-        cols = dot(rows_added(rim).astype(jnp.bfloat16), pick_ref[...])
-        first = rows[0][:, :LANES]
-        last = pltpu.roll(rows[2][:, CELLS - LANES :], 2 * TS, 1)
-        edge = jnp.where(blk < TS, first, jnp.where(blk < 2 * TS, last, cols))
+        sides.append(rows_added(rim).astype(jnp.bfloat16))
         c0 = rim[0][:, :LANES]
         c2 = rim[2][:, CELLS - LANES :]
         corner = jnp.where(blk == 0, c0, 0.0)
         corner += jnp.where(blk == TS, pltpu.roll(c0, 1, 1), 0.0)
         corner += jnp.where(blk == 2 * TS, pltpu.roll(c2, LANES - TS, 1), 0.0)
         corner += jnp.where(blk == 3 * TS, pltpu.roll(c2, LANES - TS + 1, 1), 0.0)
-        p_ref[t, :, :LANES] = edge.astype(jnp.bfloat16)
-        p_ref[t, :, LANES:] = corner.astype(jnp.bfloat16)
+        kept.append((rows[0][:, :LANES], rows[2][:, CELLS - LANES :], corner))
+    cols = dot(jnp.concatenate(sides, axis=0), pick_ref[...])
+    for t in range(tiles):
+        first, last, corner = kept[t]
+        edge = jnp.where(
+            blk < TS,
+            first,
+            jnp.where(blk < 2 * TS, pltpu.roll(last, 2 * TS, 1), cols[t * 16 : (t + 1) * 16]),
+        )
+        both = jnp.concatenate([edge, corner], axis=1)
+        p_all[base + step * tiles + t] = both.astype(jnp.bfloat16)
+
+    @pl.when(step == 0)
+    def _():
+        pl.semaphore_wait(barrier, tile_size - 1)
+        for j in range(1, tile_size):
+            edges_copy(j).start()
+
+    for j in range(1, tile_size):
+        rims_copy(j, step).start()
+
+    @pl.when(step == steps - 1)
+    def _():
+        for j in range(1, tile_size):
+            edges_copy(j).wait()
+            for i in range(steps):
+                rims_copy(j, i).wait()
+        edges_ref[...] = q_all[...]
+        rims_ref[...] = p_all[...]
 
 
 def front_kernel(
@@ -350,33 +404,43 @@
     def block(*dims):
         return pl.BlockSpec((tiles, *dims), lambda i, *_: (i,) + (0,) * len(dims))
 
-    edges = pl.pallas_call(
-        edges_kernel,
-        out_shape=jax.ShapeDtypeStruct((slots, in_chans, LANES), bf16),
-        in_specs=[vmem, vmem],
-        out_specs=vmem,
-        compiler_params=params(),
-        cost_estimate=cost(slots * 16 * CELLS * 256, slots * 16 * CELLS * 2),
-        name="edges",
-    )(x, pick)
-    all_edges = lax.all_gather(edges, "tile", axis=0, tiled=True)
-    total = all_edges.shape[0]
-
+    tile_size, dp_size = lax.axis_size("tile"), lax.axis_size("dp")
+    total = tile_size * slots
     wt = weights.transpose(2, 3, 1, 0).reshape(9 * in_chans, out_chans)
-    inner, rim_cot = pl.pallas_call(
-        back_kernel,
-        grid=(steps,),
+    back_tiles = 6
+    back_steps = slots // back_tiles
+    inner, all_edges, all_rims = pl.pallas_call(
+        lambda *refs: gather_kernel(tile_size, *refs),
+        grid=(back_steps,),
         out_shape=(
             jax.ShapeDtypeStruct((slots, in_chans, cells), f32),
-            jax.ShapeDtypeStruct((slots, in_chans, 2 * LANES), bf16),
+            jax.ShapeDtypeStruct((total, in_chans, LANES), bf16),
+            jax.ShapeDtypeStruct((total, in_chans, 2 * LANES), bf16),
         ),
-        in_specs=[block(out_chans, cells), whole(*wt.shape), whole(*pick.shape)],
-        out_specs=(block(in_chans, cells), block(in_chans, 2 * LANES)),
-        compiler_params=params(),
-        cost_estimate=cost(slots * 1024 * 144 * 128 * 8, slots * 64 * CELLS * 4),
+        in_specs=[
+            whole(slots, in_chans, cells),
+            pl.BlockSpec((back_tiles, out_chans, cells), lambda i: (i, 0, 0)),
+            whole(*wt.shape),
+            whole(*pick.shape),
+        ],
+        out_specs=(
+            pl.BlockSpec((back_tiles, in_chans, cells), lambda i: (i, 0, 0)),
+            whole(total, in_chans, LANES),
+            whole(total, in_chans, 2 * LANES),
+        ),
+        scratch_shapes=[
+            pltpu.VMEM((total, in_chans, LANES), bf16),
+            pltpu.VMEM((total, in_chans, 2 * LANES), bf16),
+            pltpu.SemaphoreType.DMA((tile_size,)),
+            pltpu.SemaphoreType.DMA((tile_size,)),
+            pltpu.SemaphoreType.DMA((tile_size, back_steps)),
+            pltpu.SemaphoreType.DMA((tile_size, back_steps)),
+        ],
+        compiler_params=pltpu.CompilerParams(
+            collective_id=1, has_side_effects=True, vmem_limit_bytes=VMEM_LIMIT
+        ),
         name="back",
-    )(g, wt, pick)
-    all_rims = lax.all_gather(rim_cot, "tile", axis=0, tiled=True)
+    )(x, g, wt, pick)
 
     slot_nbr, edge_code, flip_code = slot_tables(tile_map, neighbours, rotations)
     base = lax.axis_index("tile") * slots
@@ -422,7 +486,6 @@
     factor = 1.0 / math.sqrt(
         batch_loc * lax.axis_size("dp") * slots * lax.axis_size("tile") * cells
     )
-    dp_size, tile_size = lax.axis_size("dp"), lax.axis_size("tile")
     packed_rows = out_chans + out_chans // 4
     sums = pl.pallas_call(
         lambda *refs: sum_kernel(dp_size, tile_size, factor, *refs),

time: 68.2 us -> 56.3 us (0.83)
  blocking collectives: 13.2 us -> 0 us
  Pallas kernels: 40.4 us -> 42.6 us
  local copies, waits for them, and re-layouts: 7.55 us -> 6.61 us
    all_gather x2 -> x0, blocking collectives: 13.2 us -> none  [the longest x1 6.76 us: body(): all_rims = lax.all_gather(rim_cot, 'tile', axis=0, tiled=True)]
    pallas_call x2 -> x1, Pallas kernels: 10.3 us -> 13.3 us  [body(): pl.pallas_call(lambda *refs: gather_kernel(tile_size, *refs), grid=(back_...]
    unnamed x16 -> x14, local copies, waits for them, and re-layouts: 3.81 us -> 2.87 us
    pallas_call x1, Pallas kernels: 14.7 us -> 14 us  [body(): pl.pallas_call(lambda *refs: sum_kernel(dp_size, tile_size, factor, *refs...]
where the time goes in v3:
time: 56.3 us; the launch traced here: 55.7 us
  Pallas kernels  42.6 us (76%)
  local copies, waits for them, and re-layouts  6.61 us (12%)
  other arithmetic  5.77 us (10%)
  between operations  0.74 us (1%)
    pallas_call x1, Pallas kernels, body(): pl.pallas_call(lambda *refs: sum_kernel(dp_size, tile_size, factor, *refs...  14 us
    pallas_call x1, Pallas kernels, body(): pl.pallas_call(lambda *refs: gather_kernel(tile_size, *refs), grid=(back_...  13.3 us
    pallas_call x1, Pallas kernels, body(): pl.pallas_call(lambda *refs: front_kernel(slots, *refs), grid_spec=pltpu....  10.7 us
    pallas_call x1, Pallas kernels, body(): pl.pallas_call(lambda *refs: finish_kernel(slots, *refs), out_shape=jax.S...  4.63 us
    unnamed x14, local copies, waits for them, and re-layouts  2.87 us
    reduce_sum x1, other arithmetic, slot_tables(): tile_rot = jnp.sum(onehot[:, :, None] * rotations[None], axis=1)  2.4 us

profile of v3, /device:TPU:0, one launch (start us, length us, event | category | flops | bytes accessed | tf_op | source)
XLA Modules:
  0.0 55.7 jit_solution(10263584107538080306)
XLA Ops:
  0.6 0.0 copy-start.5
  0.6 0.8 %select_reduce_fusion.1 = s32[48]{0:T(128)S(1)} fusion(s32[48]{0:T(128)} %param.19), kind=kLoop, calls=%fused_computation.5 | loop fusion | flops 6864 | bytes 384 | tf_op jit(solution)/shard_map/reduce_sum | solution.py:46
  1.5 0.7 %fusion = s32[48,48]{1,0:T(8,128)S(1)} fusion(s32[48]{0:T(128)} %param.19), kind=kLoop, calls=%fused_computation.8 | loop fusion | flops 4608 | bytes 9408 | tf_op jit(solution)/shard_map/convert_element_type | solution.py:45
  2.2 2.4 %multiply_reduce_fusion.1 = (s32[48,8]{1,0:T(8,128)S(1)}, s32[48,8]{1,0:T(8,128)S(1)}) fusion(s32[48,8]{0,1:T(8,128)} %param.18, s32[48,48]{1,0:T(8,128)S(1)} %fusion, s32[48,8]{0,1:T(8,128)} %param.17), kind=kLoop, calls=%fused_computation.3 | loop fusion | flops 72960 | bytes 15360 | tf_op jit(solution)/shard_map/reduce_sum | solution.py:50
  4.6 0.1 copy.27
  4.7 0.8 %select_reduce_fusion.3 = (s32[48,8]{0,1:T(8,128)S(1)}, s32[48,8]{0,1:T(8,128)S(1)}) fusion(s32[8,4]{0,1:T(4,128)} %constant.38.clone, s32[48,8]{0,1:T(8,128)S(1)} %copy.27, s32[8,4]{0,1:T(4,128)} %constant.39.clone), kind=kLoop, calls=%fused_computation.10 | loop fusion | flops 6912 | bytes 4864 | tf_op jit(solution)/shard_map/reduce_sum | solution.py:56
  5.5 1.0 %select_reduce_fusion = s32[48,8]{1,0:T(8,128)S(1)} fusion(s32[48]{0:T(128)S(1)} %select_reduce_fusion.1, s32[48,8]{1,0:T(8,128)S(1)} %get-tuple-element.15), kind=kLoop, calls=%fused_computation | loop fusion | flops 54912 | bytes 3264 | tf_op jit(solution)/shard_map/reduce_sum | solution.py:51
  6.4 0.1 copy.28
  6.5 0.1 add_select_fusion
  6.6 0.1 constant_dynamic-slice_fusion
  6.6 0.1 copy.29
  6.7 0.1 reshape.90.refs_0_
  6.8 0.1 copy.34
  6.9 0.1 select_n.13.refs_1_
  7.0 0.1 copy.32
  7.1 0.1 add.43.refs_0_
  7.2 0.7 %copy.31.refs_7_ = f32[64,1]{1,0:T(8,128)S(1)} copy(f32[64,1]{0,1:T(1,128)} %bitcast.23) | data formatting | bytes 512 | tf_op jit(solution)/shard_map/broadcast_in_dim | solution.py:485
  7.9 0.8 %copy.30.refs_6_ = bf16[64,144]{1,0:T(8,128)(2,1)S(1)} copy(bf16[64,144]{0,1:T(8,128)(2,1)} %bitcast.18) | data formatting | bytes 36864 | tf_op jit(solution)/shard_map/reshape | solution.py:454
  8.8 0.0 copy-start
  8.8 1.1 %copy-done = bf16[1,24,16,1024]{3,2,1,0:T(8,128)(2,1)S(1)} copy-done((bf16[1,24,16,1024]{3,2,1,0:T(8,128)(2,1)S(1)}, bf16[1,24,16,1024]{3,2,1,0:T(8,128)(2,1)}, u32[]{:S(2)}) %copy-start) | copy-done | bytes 786456
  9.9 0.9 %copy-done.2 = bf16[1024,128]{1,0:T(8,128)(2,1)S(1)} copy-done((bf16[1024,128]{1,0:T(8,128)(2,1)S(1)}, bf16[1024,128]{1,0:T(8,128)(2,1)}, u32[]{:S(2)}) %copy-start.2) | copy-done | bytes 262168
  10.9 0.8 %copy-done.3 = bf16[64,16,3,3]{0,1,3,2:T(8,128)(2,1)S(1)} copy-done((bf16[64,16,3,3]{0,1,3,2:T(8,128)(2,1)S(1)}, bf16[64,16,3,3]{0,1,3,2:T(8,128)(2,1)}, u32[]{:S(2)}) %copy-start.3) | copy-done | bytes 18456
  11.6 13.3 %back.1 = (f32[24,16,1024]{2,1,0:T(8,128)S(1)}, bf16[48,16,128]{2,1,0:T(8,128)(2,1)S(1)}, bf16[48,16,256]{2,1,0:T(8,128)(2,1)S(1)}) custom-call(bf16[24,16,1024]{2,1,0:T(8,128)(2,1)S(1)} %bitcast.15, bf16[24,64,1024]{2,1,0:T(8,128)(2,1)} %bitcast.20, bf16[144,64]{1,0:T(8,128)(2,1)S(1)} %bitcast.19, bf16[1024,128]{1,0:T(8,128)(2,1)S(1)} %copy-done.2), custom_call_target="tpu_custom_call" | custom-call | tf_op jit(solution)/shard_map/back/pallas_call | solution.py:412
  24.9 0.0 copy-done.5
  24.9 0.0 copy-done.6
  24.9 0.0 copy-start.1
  24.9 0.0 copy-start.4
  24.9 4.6 %finish.1 = bf16[24,16,1024]{2,1,0:T(8,128)(2,1)} custom-call(s32[384]{0:T(512)S(1)} %add.43.refs_0_, s32[384]{0:T(512)S(1)} %select_n.13.refs_1_, bf16[48,16,256]{2,1,0:T(8,128)(2,1)S(1)} %get-tuple-element.11.refs_2_, bf16[128,1024]{1,0:T(8,128)(2,1)S(1)} %copy-done.6, bf16[256,1024]{1,0:T(8,128)(2,1)S(1)} %copy-done.5, ...), custom_call_target="tpu_custom_call" | custom-call | flops 3623878656 | bytes 6291456 | tf_op jit(solution)/shard_map/finish/pallas_call | solution.py:512
  29.6 10.7 %front.1 = (bf16[24,64,1024]{2,1,0:T(8,128)(2,1)}, f32[64,160]{1,0:T(8,128)S(1)}) custom-call(s32[192]{0:T(256)S(1)} %reshape.90.refs_0_, bf16[48,16,128]{2,1,0:T(8,128)(2,1)S(1)} %get-tuple-element.9.refs_1_, bf16[128,1024]{1,0:T(8,128)(2,1)S(1)} %copy-done.6, bf16[256,1408]{1,0:T(8,128)(2,1)S(1)} %copy-done.4, bf16[24,16,1024]{2,1,0:T(8,128)(2,1)S(1)} %bitcast.16, ...), custom_call_target="tpu_custom_call" | custom-call | flops 7247757312 | bytes 6291456 | tf_op jit(solution)/shard_map/front/pallas_call | solution.py:456
  40.3 14.0 %sums.1 = f32[64,160]{1,0:T(8,128)S(1)} custom-call(f32[64,160]{1,0:T(8,128)S(1)} %get-tuple-element.13.refs_0_), custom_call_target="tpu_custom_call" | custom-call | tf_op jit(solution)/shard_map/sums/pallas_call | solution.py:490
  54.3 0.7 %slice_reduce_fusion = f32[64]{0:T(128)} fusion(f32[64,160]{1,0:T(8,128)S(1)} %sums.1), kind=kLoop, calls=%fused_computation.4 | loop fusion | bytes 512 | tf_op jit(solution)/shard_map/slice | solution.py:509
  55.0 0.7 %copy.35 = f32[64,144]{0,1:T(8,128)} copy(f32[64,144]{1,0:T(8,128)S(1)} %bitcast.17) | data formatting | bytes 73728 | tf_op jit(solution)/shard_map/slice | solution.py:508
  (6 shorter events, 0.0 us)
Async XLA Ops:
  0.6 24.3 %copy-start.5 = (bf16[256,1024]{1,0:T(8,128)(2,1)S(1)}, bf16[256,1024]{1,0:T(8,128)(2,1)}, u32[]{:S(2)}) copy-start(bf16[256,1024]{1,0:T(8,128)(2,1)} %constant.41.clone.refs_4_) | copy-start | bytes 1572868
  8.8 1.1 %copy-start = (bf16[1,24,16,1024]{3,2,1,0:T(8,128)(2,1)S(1)}, bf16[1,24,16,1024]{3,2,1,0:T(8,128)(2,1)}, u32[]{:S(2)}) copy-start(bf16[1,24,16,1024]{3,2,1,0:T(8,128)(2,1)} %param.13) | copy-start | bytes 2359300
  9.9 0.9 %copy-start.2 = (bf16[1024,128]{1,0:T(8,128)(2,1)S(1)}, bf16[1024,128]{1,0:T(8,128)(2,1)}, u32[]{:S(2)}) copy-start(bf16[1024,128]{1,0:T(8,128)(2,1)} %constant.36.clone.refs_3_) | copy-start | bytes 786436
  10.9 0.8 %copy-start.3 = (bf16[64,16,3,3]{0,1,3,2:T(8,128)(2,1)S(1)}, bf16[64,16,3,3]{0,1,3,2:T(8,128)(2,1)}, u32[]{:S(2)}) copy-start(bf16[64,16,3,3]{0,1,3,2:T(8,128)(2,1)} %param.14) | copy-start | bytes 55300
  11.6 13.3 %copy-start.6 = (bf16[128,1024]{1,0:T(8,128)(2,1)S(1)}, bf16[128,1024]{1,0:T(8,128)(2,1)}, u32[]{:S(2)}) copy-start(bf16[128,1024]{1,0:T(8,128)(2,1)} %constant.37.clone.refs_2_.refs_3_) | copy-start | bytes 786436
  24.9 4.7 %copy-start.1 = (bf16[1,24,16,1024]{3,2,1,0:T(8,128)(2,1)S(1)}, bf16[1,24,16,1024]{3,2,1,0:T(8,128)(2,1)}, u32[]{:S(2)}) copy-start(bf16[1,24,16,1024]{3,2,1,0:T(8,128)(2,1)} %param.13) | copy-start | bytes 2359300
  24.9 4.7 %copy-start.4 = (bf16[256,1408]{1,0:T(8,128)(2,1)S(1)}, bf16[256,1408]{1,0:T(8,128)(2,1)}, u32[]{:S(2)}) copy-start(bf16[256,1408]{1,0:T(8,128)(2,1)} %constant.40.clone.refs_3_) | copy-start | bytes 2162692

commit v4 on v3

--- a/solution.py
+++ b/solution.py
@@ -315,22 +315,32 @@
     out_ref[...] = out.astype(jnp.bfloat16).reshape(slots, 16, CELLS)
 
 
-def sum_kernel(dp_size, tile_size, factor, in_ref, out_ref, near_ref, far_ref, near_send, near_recv, far_send, far_recv):
+def sum_kernel(
+    dp_size, tile_size, factor, in_ref, out_ref, src_ref, near_ref, far_ref, all_ref,
+    near_send, near_recv, far_send, far_recv, all_send, all_recv,
+):
     dp, tile = lax.axis_index("dp"), lax.axis_index("tile")
     pairs = dp_size // 2
     core, hi = lax.rem(dp, 2), dp // 2
     near_count = 2 * tile_size
+    chunk = src_ref.shape[1]
+    me = core * tile_size + tile
+    mesh_ids = pl.DeviceIdType.MESH
 
     def near_peer(j):
-        return (hi * 2 + lax.rem(core + j % 2, 2), lax.rem(tile + j // 2, tile_size))
-
-    def far_peer(j):
+        return (lax.rem(core + j % 2, 2), lax.rem(tile + j // 2, tile_size))
+
+    def near_device(j):
+        peer_core, peer_tile = near_peer(j)
+        return (hi * 2 + peer_core, peer_tile)
+
+    def far_device(j):
         return (lax.rem(hi + j, pairs) * 2 + core, tile)
 
-    peers = [near_peer(j) for j in range(1, near_count)] + [far_peer(j) for j in range(1, pairs)]
+    peers = [near_device(j) for j in range(1, near_count)] + [far_device(j) for j in range(1, pairs)]
     barrier = pltpu.get_barrier_semaphore()
     for peer in peers:
-        pl.semaphore_signal(barrier, inc=1, device_id=peer, device_id_type=pl.DeviceIdType.MESH)
+        pl.semaphore_signal(barrier, inc=1, device_id=peer, device_id_type=mesh_ids)
 
     rows = in_ref.shape[0]
     quarter = rows // 4
@@ -339,41 +349,57 @@
         [
             in_ref[:, :LANES],
             jnp.concatenate([rest[k * quarter : (k + 1) * quarter] for k in range(4)], axis=1),
+            jnp.zeros((near_count * chunk - rows - quarter, LANES), jnp.float32),
         ],
         axis=0,
     )
+    src_ref[...] = packed.reshape(near_count, chunk, LANES)
+    near_ref[me] = src_ref[me]
     pl.semaphore_wait(barrier, len(peers))
 
-    def exchange(value, ref, me, count, peer_of, send, recv):
-        ref[me] = value
+    def exchange(count, src_of, dst, device_of, send, recv):
         copies = []
         for j in range(1, count):
             copy = pltpu.make_async_remote_copy(
-                src_ref=ref.at[me],
-                dst_ref=ref.at[me],
+                src_ref=src_of(j),
+                dst_ref=dst,
                 send_sem=send.at[j],
                 recv_sem=recv.at[j],
-                device_id=peer_of(j),
-                device_id_type=pl.DeviceIdType.MESH,
+                device_id=device_of(j),
+                device_id_type=mesh_ids,
             )
             copy.start()
             copies.append(copy)
         for copy in copies:
             copy.wait_recv()
+        return copies
+
+    def added(ref):
         total = ref[0]
-        for j in range(1, count):
+        for j in range(1, ref.shape[0]):
             total = total + ref[j]
-        return total, copies
-
-    near, near_copies = exchange(
-        packed, near_ref, core * tile_size + tile, near_count, near_peer, near_send, near_recv
-    )
-    far, far_copies = exchange(near, far_ref, hi, pairs, far_peer, far_send, far_recv)
-    far = far * factor
-    out_ref[:, :LANES] = far[:rows]
+        return total
+
+    def chunk_for(j):
+        peer_core, peer_tile = near_peer(j)
+        return src_ref.at[peer_core * tile_size + peer_tile]
+
+    copies = exchange(near_count, chunk_for, near_ref.at[me], near_device, near_send, near_recv)
+    far_ref[hi] = added(near_ref)
+    copies += exchange(
+        pairs, lambda j: far_ref.at[hi], far_ref.at[hi], far_device, far_send, far_recv
+    )
+    all_ref[me] = added(far_ref) * factor
+    copies += exchange(
+        near_count, lambda j: all_ref.at[me], all_ref.at[me], near_device, all_send, all_recv
+    )
+    whole = all_ref[...].reshape(near_count * chunk, LANES)
+    out_ref[:, :LANES] = whole[:rows]
     for k in range(4):
-        out_ref[k * quarter : (k + 1) * quarter, LANES:] = far[rows:, k * 32 : (k + 1) * 32]
-    for copy in near_copies + far_copies:
+        out_ref[k * quarter : (k + 1) * quarter, LANES:] = whole[
+            rows : rows + quarter, k * 32 : (k + 1) * 32
+        ]
+    for copy in copies:
         copy.wait_send()
 
 
@@ -486,19 +512,25 @@
     factor = 1.0 / math.sqrt(
         batch_loc * lax.axis_size("dp") * slots * lax.axis_size("tile") * cells
     )
+    near_count, pairs = 2 * tile_size, dp_size // 2
     packed_rows = out_chans + out_chans // 4
+    chunk = -(-packed_rows // (8 * near_count)) * 8
     sums = pl.pallas_call(
         lambda *refs: sum_kernel(dp_size, tile_size, factor, *refs),
         out_shape=jax.ShapeDtypeStruct((out_chans, 160), f32),
         in_specs=[vmem],
         out_specs=vmem,
         scratch_shapes=[
-            pltpu.VMEM((2 * tile_size, packed_rows, LANES), f32),
-            pltpu.VMEM((dp_size // 2, packed_rows, LANES), f32),
-            pltpu.SemaphoreType.DMA((2 * tile_size,)),
-            pltpu.SemaphoreType.DMA((2 * tile_size,)),
-            pltpu.SemaphoreType.DMA((dp_size // 2,)),
-            pltpu.SemaphoreType.DMA((dp_size // 2,)),
+            pltpu.VMEM((near_count, chunk, LANES), f32),
+            pltpu.VMEM((near_count, chunk, LANES), f32),
+            pltpu.VMEM((pairs, chunk, LANES), f32),
+            pltpu.VMEM((near_count, chunk, LANES), f32),
+            pltpu.SemaphoreType.DMA((near_count,)),
+            pltpu.SemaphoreType.DMA((near_count,)),
+            pltpu.SemaphoreType.DMA((pairs,)),
+            pltpu.SemaphoreType.DMA((pairs,)),
+            pltpu.SemaphoreType.DMA((near_count,)),
+            pltpu.SemaphoreType.DMA((near_count,)),
         ],
         compiler_params=pltpu.CompilerParams(
             collective_id=0, has_side_effects=True, vmem_limit_bytes=VMEM_LIMIT

time: 56.3 us -> 55.5 us (0.986)
  Pallas kernels: 42.6 us -> 41.8 us
    pallas_call x1, Pallas kernels: 14 us -> 13.2 us  [body(): pl.pallas_call(lambda *refs: sum_kernel(dp_size, tile_size, factor, *refs...]
where the time goes in v4:
time: 55.5 us; the launch traced here: 54.9 us
  Pallas kernels  41.8 us (75%)
  local copies, waits for them, and re-layouts  6.61 us (12%)
  other arithmetic  5.77 us (10%)
  between operations  0.74 us (1%)
    pallas_call x1, Pallas kernels, body(): pl.pallas_call(lambda *refs: gather_kernel(tile_size, *refs), grid=(back_...  13.3 us
    pallas_call x1, Pallas kernels, body(): pl.pallas_call(lambda *refs: sum_kernel(dp_size, tile_size, factor, *refs...  13.2 us
    pallas_call x1, Pallas kernels, body(): pl.pallas_call(lambda *refs: front_kernel(slots, *refs), grid_spec=pltpu....  10.7 us
    pallas_call x1, Pallas kernels, body(): pl.pallas_call(lambda *refs: finish_kernel(slots, *refs), out_shape=jax.S...  4.63 us
    unnamed x14, local copies, waits for them, and re-layouts  2.87 us
    reduce_sum x1, other arithmetic, slot_tables(): tile_rot = jnp.sum(onehot[:, :, None] * rotations[None], axis=1)  2.4 us

profile of v4, /device:TPU:0, one launch (start us, length us, event | category | flops | bytes accessed | tf_op | source)
XLA Modules:
  0.0 54.9 jit_solution(1334999542440964988)
XLA Ops:
  0.6 0.0 copy-start.5
  0.6 0.8 %select_reduce_fusion.1 = s32[48]{0:T(128)S(1)} fusion(s32[48]{0:T(128)} %param.19), kind=kLoop, calls=%fused_computation.5 | loop fusion | flops 6864 | bytes 384 | tf_op jit(solution)/shard_map/reduce_sum | solution.py:46
  1.5 0.7 %fusion = s32[48,48]{1,0:T(8,128)S(1)} fusion(s32[48]{0:T(128)} %param.19), kind=kLoop, calls=%fused_computation.8 | loop fusion | flops 4608 | bytes 9408 | tf_op jit(solution)/shard_map/convert_element_type | solution.py:45
  2.2 2.4 %multiply_reduce_fusion.1 = (s32[48,8]{1,0:T(8,128)S(1)}, s32[48,8]{1,0:T(8,128)S(1)}) fusion(s32[48,8]{0,1:T(8,128)} %param.18, s32[48,48]{1,0:T(8,128)S(1)} %fusion, s32[48,8]{0,1:T(8,128)} %param.17), kind=kLoop, calls=%fused_computation.3 | loop fusion | flops 72960 | bytes 15360 | tf_op jit(solution)/shard_map/reduce_sum | solution.py:50
  4.6 0.1 copy.27
  4.7 0.8 %select_reduce_fusion.3 = (s32[48,8]{0,1:T(8,128)S(1)}, s32[48,8]{0,1:T(8,128)S(1)}) fusion(s32[8,4]{0,1:T(4,128)} %constant.38.clone, s32[48,8]{0,1:T(8,128)S(1)} %copy.27, s32[8,4]{0,1:T(4,128)} %constant.39.clone), kind=kLoop, calls=%fused_computation.10 | loop fusion | flops 6912 | bytes 4864 | tf_op jit(solution)/shard_map/reduce_sum | solution.py:56
  5.5 1.0 %select_reduce_fusion = s32[48,8]{1,0:T(8,128)S(1)} fusion(s32[48]{0:T(128)S(1)} %select_reduce_fusion.1, s32[48,8]{1,0:T(8,128)S(1)} %get-tuple-element.15), kind=kLoop, calls=%fused_computation | loop fusion | flops 54912 | bytes 3264 | tf_op jit(solution)/shard_map/reduce_sum | solution.py:51
  6.4 0.1 copy.28
  6.5 0.1 add_select_fusion
  6.6 0.1 constant_dynamic-slice_fusion
  6.6 0.1 copy.29
  6.7 0.1 reshape.90.refs_0_
  6.8 0.1 copy.34
  6.9 0.1 select_n.13.refs_1_
  7.0 0.1 copy.32
  7.1 0.1 add.43.refs_0_
  7.2 0.7 %copy.31.refs_7_ = f32[64,1]{1,0:T(8,128)S(1)} copy(f32[64,1]{0,1:T(1,128)} %bitcast.23) | data formatting | bytes 512 | tf_op jit(solution)/shard_map/broadcast_in_dim | solution.py:511
  7.9 0.8 %copy.30.refs_6_ = bf16[64,144]{1,0:T(8,128)(2,1)S(1)} copy(bf16[64,144]{0,1:T(8,128)(2,1)} %bitcast.18) | data formatting | bytes 36864 | tf_op jit(solution)/shard_map/reshape | solution.py:480
  8.8 0.0 copy-start
  8.8 1.1 %copy-done = bf16[1,24,16,1024]{3,2,1,0:T(8,128)(2,1)S(1)} copy-done((bf16[1,24,16,1024]{3,2,1,0:T(8,128)(2,1)S(1)}, bf16[1,24,16,1024]{3,2,1,0:T(8,128)(2,1)}, u32[]{:S(2)}) %copy-start) | copy-done | bytes 786456
  9.9 0.9 %copy-done.2 = bf16[1024,128]{1,0:T(8,128)(2,1)S(1)} copy-done((bf16[1024,128]{1,0:T(8,128)(2,1)S(1)}, bf16[1024,128]{1,0:T(8,128)(2,1)}, u32[]{:S(2)}) %copy-start.2) | copy-done | bytes 262168
  10.9 0.8 %copy-done.3 = bf16[64,16,3,3]{0,1,3,2:T(8,128)(2,1)S(1)} copy-done((bf16[64,16,3,3]{0,1,3,2:T(8,128)(2,1)S(1)}, bf16[64,16,3,3]{0,1,3,2:T(8,128)(2,1)}, u32[]{:S(2)}) %copy-start.3) | copy-done | bytes 18456
  11.6 13.3 %back.1 = (f32[24,16,1024]{2,1,0:T(8,128)S(1)}, bf16[48,16,128]{2,1,0:T(8,128)(2,1)S(1)}, bf16[48,16,256]{2,1,0:T(8,128)(2,1)S(1)}) custom-call(bf16[24,16,1024]{2,1,0:T(8,128)(2,1)S(1)} %bitcast.15, bf16[24,64,1024]{2,1,0:T(8,128)(2,1)} %bitcast.20, bf16[144,64]{1,0:T(8,128)(2,1)S(1)} %bitcast.19, bf16[1024,128]{1,0:T(8,128)(2,1)S(1)} %copy-done.2), custom_call_target="tpu_custom_call" | custom-call | tf_op jit(solution)/shard_map/back/pallas_call | solution.py:438
  24.9 0.0 copy-done.5
  24.9 0.0 copy-start.1
  24.9 0.0 copy-start.4
  24.9 4.6 %finish.1 = bf16[24,16,1024]{2,1,0:T(8,128)(2,1)} custom-call(s32[384]{0:T(512)S(1)} %add.43.refs_0_, s32[384]{0:T(512)S(1)} %select_n.13.refs_1_, bf16[48,16,256]{2,1,0:T(8,128)(2,1)S(1)} %get-tuple-element.11.refs_2_, bf16[128,1024]{1,0:T(8,128)(2,1)S(1)} %copy-done.6, bf16[256,1024]{1,0:T(8,128)(2,1)S(1)} %copy-done.5, ...), custom_call_target="tpu_custom_call" | custom-call | flops 3623878656 | bytes 6291456 | tf_op jit(solution)/shard_map/finish/pallas_call | solution.py:544
  29.6 0.0 copy-done.1
  29.6 10.7 %front.1 = (bf16[24,64,1024]{2,1,0:T(8,128)(2,1)}, f32[64,160]{1,0:T(8,128)S(1)}) custom-call(s32[192]{0:T(256)S(1)} %reshape.90.refs_0_, bf16[48,16,128]{2,1,0:T(8,128)(2,1)S(1)} %get-tuple-element.9.refs_1_, bf16[128,1024]{1,0:T(8,128)(2,1)S(1)} %copy-done.6, bf16[256,1408]{1,0:T(8,128)(2,1)S(1)} %copy-done.4, bf16[24,16,1024]{2,1,0:T(8,128)(2,1)S(1)} %bitcast.16, ...), custom_call_target="tpu_custom_call" | custom-call | flops 7247757312 | bytes 6291456 | tf_op jit(solution)/shard_map/front/pallas_call | solution.py:482
  40.3 13.2 %sums.1 = f32[64,160]{1,0:T(8,128)S(1)} custom-call(f32[64,160]{1,0:T(8,128)S(1)} %get-tuple-element.13.refs_0_), custom_call_target="tpu_custom_call" | custom-call | tf_op jit(solution)/shard_map/sums/pallas_call | solution.py:518
  53.5 0.7 %slice_reduce_fusion = f32[64]{0:T(128)} fusion(f32[64,160]{1,0:T(8,128)S(1)} %sums.1), kind=kLoop, calls=%fused_computation.4 | loop fusion | bytes 512 | tf_op jit(solution)/shard_map/slice | solution.py:541
  54.2 0.7 %copy.35 = f32[64,144]{0,1:T(8,128)} copy(f32[64,144]{1,0:T(8,128)S(1)} %bitcast.17) | data formatting | bytes 73728 | tf_op jit(solution)/shard_map/slice | solution.py:540
  (6 shorter events, 0.0 us)
Async XLA Ops:
  0.6 24.3 %copy-start.5 = (bf16[256,1024]{1,0:T(8,128)(2,1)S(1)}, bf16[256,1024]{1,0:T(8,128)(2,1)}, u32[]{:S(2)}) copy-start(bf16[256,1024]{1,0:T(8,128)(2,1)} %constant.41.clone.refs_4_) | copy-start | bytes 1572868
  8.8 1.1 %copy-start = (bf16[1,24,16,1024]{3,2,1,0:T(8,128)(2,1)S(1)}, bf16[1,24,16,1024]{3,2,1,0:T(8,128)(2,1)}, u32[]{:S(2)}) copy-start(bf16[1,24,16,1024]{3,2,1,0:T(8,128)(2,1)} %param.13) | copy-start | bytes 2359300
  9.9 0.9 %copy-start.2 = (bf16[1024,128]{1,0:T(8,128)(2,1)S(1)}, bf16[1024,128]{1,0:T(8,128)(2,1)}, u32[]{:S(2)}) copy-start(bf16[1024,128]{1,0:T(8,128)(2,1)} %constant.36.clone.refs_3_) | copy-start | bytes 786436
  10.9 0.8 %copy-start.3 = (bf16[64,16,3,3]{0,1,3,2:T(8,128)(2,1)S(1)}, bf16[64,16,3,3]{0,1,3,2:T(8,128)(2,1)}, u32[]{:S(2)}) copy-start(bf16[64,16,3,3]{0,1,3,2:T(8,128)(2,1)} %param.14) | copy-start | bytes 55300
  11.6 13.3 %copy-start.6 = (bf16[128,1024]{1,0:T(8,128)(2,1)S(1)}, bf16[128,1024]{1,0:T(8,128)(2,1)}, u32[]{:S(2)}) copy-start(bf16[128,1024]{1,0:T(8,128)(2,1)} %constant.37.clone.refs_2_.refs_3_) | copy-start | bytes 786436
  24.9 4.7 %copy-start.1 = (bf16[1,24,16,1024]{3,2,1,0:T(8,128)(2,1)S(1)}, bf16[1,24,16,1024]{3,2,1,0:T(8,128)(2,1)}, u32[]{:S(2)}) copy-start(bf16[1,24,16,1024]{3,2,1,0:T(8,128)(2,1)} %param.13) | copy-start | bytes 2359300
  24.9 4.7 %copy-start.4 = (bf16[256,1408]{1,0:T(8,128)(2,1)S(1)}, bf16[256,1408]{1,0:T(8,128)(2,1)}, u32[]{:S(2)}) copy-start(bf16[256,1408]{1,0:T(8,128)(2,1)} %constant.40.clone.refs_3_) | copy-start | bytes 2162692

commit v5 on v4

--- a/solution.py
+++ b/solution.py
@@ -39,23 +39,34 @@
 )
 
 
-def slot_tables(tile_map, neighbours, rotations):
-    total_slots = tile_map.shape[0]
-    places = jnp.arange(total_slots, dtype=jnp.int32)
-    onehot = (tile_map[:, None] == places[None, :]).astype(jnp.int32)
-    inverse = jnp.sum(
-        (tile_map[None, :] == places[:, None]).astype(jnp.int32) * places[None, :], axis=1
-    )
-    tile_nbr = jnp.sum(onehot[:, :, None] * neighbours[None], axis=1)
-    tile_rot = jnp.sum(onehot[:, :, None] * rotations[None], axis=1)
-    slot_nbr = jnp.sum(
-        (tile_nbr[:, :, None] == places[None, None, :]).astype(jnp.int32) * inverse[None, None, :],
-        axis=2,
-    )
-    matches = (tile_rot[:, :, None] == jnp.arange(4, dtype=jnp.int32)).astype(jnp.int32)
-    edge_code = jnp.sum(matches * jnp.asarray(edge_table)[None], axis=-1)
-    flip_code = jnp.sum(matches * jnp.asarray(flip_table)[None], axis=-1)
-    return (slot_nbr, edge_code, flip_code)
+def tables_kernel(slots, map_ref, nbr_ref, rot_ref, fsrc_ref, bsrc_ref, bdst_ref):
+    total = map_ref.shape[1]
+    base = lax.axis_index("tile") * slots
+    held = map_ref[...].astype(jnp.float32)
+    rows = lax.broadcasted_iota(jnp.int32, (total, total), 0)
+    cols = lax.broadcasted_iota(jnp.int32, (total, total), 1)
+    places = cols.astype(jnp.float32)
+    held_col = jnp.sum(jnp.where(rows == cols, held, 0.0), axis=1, keepdims=True)
+    onehot = jnp.where(held_col == places, 1.0, 0.0).astype(jnp.bfloat16)
+    tile_nbr = dot(onehot, nbr_ref[...].astype(jnp.float32).astype(jnp.bfloat16))
+    tile_rot = dot(onehot, rot_ref[...].astype(jnp.float32).astype(jnp.bfloat16))
+    k_ids = lax.broadcasted_iota(jnp.int32, (total, 8), 1)
+    s_ids = lax.broadcasted_iota(jnp.int32, (total, 8), 0)
+    nbr = jnp.zeros((total, 8), jnp.float32)
+    edge = jnp.zeros((total, 8), jnp.int32)
+    flip = jnp.zeros((total, 8), jnp.int32)
+    for k in range(8):
+        found = jnp.where(held == tile_nbr[:, k : k + 1], places, 0.0)
+        nbr = jnp.where(k_ids == k, jnp.sum(found, axis=1, keepdims=True), nbr)
+        for r in range(4):
+            here = (k_ids == k) & (tile_rot == float(r))
+            edge = jnp.where(here, int(edge_table[k, r]), edge)
+            flip = jnp.where(here, int(flip_table[k, r]), flip)
+    nbr = nbr.astype(jnp.int32)
+    fsrc_ref[...] = (edge * 2 + flip) * total + nbr
+    bsrc_ref[...] = (k_ids * 2 + flip) * total + s_ids
+    own = nbr - base
+    bdst_ref[...] = jnp.where((own >= 0) & (own < slots), own * 4 + edge, slots * 4)
 
 
 CELLS = TS * TS
@@ -229,13 +240,14 @@
     @pl.when(step == 0)
     def _():
         total = q_ref.shape[0]
+        base = lax.axis_index("tile") * slots
         q = q_ref[...].reshape(total * 16, LANES)
         for j in range(8):
             got = dot(q, var_ref[:, j * LANES : (j + 1) * LANES])
             v_ref[j * total : (j + 1) * total] = got.reshape(total, 16, LANES)
         for s in range(slots):
             for half in range(2):
-                parts = [v_ref[fsrc_ref[s * 8 + half * 4 + k]] for k in range(4)]
+                parts = [v_ref[fsrc_ref[base + s, half * 4 + k]] for k in range(4)]
                 rim = jnp.where(
                     blk < 2 * TS,
                     jnp.where(blk < TS, parts[0], parts[1]),
@@ -250,6 +262,11 @@
 
     w = lane_ids(CELLS) % TS
     tiles = x_ref.shape[0]
+    chans = bias_ref.shape[1]
+    same = lax.broadcasted_iota(jnp.int32, (chans, chans), 0) == lax.broadcasted_iota(
+        jnp.int32, (chans, chans), 1
+    )
+    bias = jnp.sum(jnp.where(same, bias_ref[...], 0.0), axis=1, keepdims=True)
     total = jnp.zeros(dw_ref.shape, jnp.float32)
     for t in range(tiles):
         s = step * tiles + t
@@ -275,7 +292,7 @@
                 row = (a * 3 + c) * 16
                 col_ref[t, row : row + 16, :] = tap.astype(jnp.bfloat16)
         col = col_ref[t]
-        out_ref[t] = (dot(w_ref[...], col[:144]) + bias_ref[...]).astype(jnp.bfloat16)
+        out_ref[t] = (dot(w_ref[...], col[:144]) + bias).astype(jnp.bfloat16)
         total += lax.dot_general(
             g_ref[t], col, (((1,), (1,)), ((), ())), preferred_element_type=jnp.float32
         )
@@ -295,8 +312,8 @@
 
     def add(q, carry):
         for k in range(8):
-            d = bdst_ref[q * 8 + k]
-            acc_ref[d] = acc_ref[d] + u_ref[bsrc_ref[q * 8 + k]]
+            d = bdst_ref[q, k]
+            acc_ref[d] = acc_ref[d] + u_ref[bsrc_ref[q, k]]
         return carry
 
     lax.fori_loop(0, total, add, 0)
@@ -468,14 +485,13 @@
         name="back",
     )(x, g, wt, pick)
 
-    slot_nbr, edge_code, flip_code = slot_tables(tile_map, neighbours, rotations)
-    base = lax.axis_index("tile") * slots
-    src = (edge_code * 2 + flip_code) * total + slot_nbr
-    fsrc = lax.dynamic_slice_in_dim(src, base, slots, 0).reshape(-1)
-    here = slot_nbr - base
-    bdst = jnp.where((here >= 0) & (here < slots), here * 4 + edge_code, slots * 4).reshape(-1)
-    ks = jnp.arange(8, dtype=jnp.int32)[None, :]
-    bsrc = ((ks * 2 + flip_code) * total + jnp.arange(total, dtype=jnp.int32)[:, None]).reshape(-1)
+    fsrc, bsrc, bdst = pl.pallas_call(
+        lambda *refs: tables_kernel(slots, *refs),
+        out_shape=(jax.ShapeDtypeStruct((total, 8), jnp.int32),) * 3,
+        in_specs=[vmem] * 3,
+        out_specs=(vmem,) * 3,
+        name="tables",
+    )(tile_map.reshape(1, total), neighbours, rotations)
 
     wf = weights.transpose(0, 2, 3, 1).reshape(out_chans, 9 * in_chans)
     images = const(rim_images())
@@ -491,7 +507,7 @@
                 block(in_chans, cells),
                 block(out_chans, cells),
                 whole(*wf.shape),
-                whole(out_chans, 1),
+                whole(1, out_chans),
             ],
             out_specs=(block(out_chans, cells), whole(out_chans, 160)),
             scratch_shapes=[
@@ -508,7 +524,7 @@
         compiler_params=params(),
         cost_estimate=cost(slots * 1024 * 144 * 256 * 8, slots * 64 * CELLS * 4),
         name="front",
-    )(fsrc, all_edges, variants, images, x, g, wf, bias[:, None])
+    )(fsrc, all_edges, variants, images, x, g, wf, bias[None, :])
     factor = 1.0 / math.sqrt(
         batch_loc * lax.axis_size("dp") * slots * lax.axis_size("tile") * cells
     )

time: 55.5 us -> 54.2 us (0.977)
  other arithmetic: 5.77 us -> 0 us
  Pallas kernels: 41.8 us -> 44.9 us
  local copies, waits for them, and re-layouts: 6.61 us -> 7.91 us
    reduce_sum x4 -> x0, other arithmetic: 4.96 us -> none  [the longest x1 2.4 us: slot_tables(): tile_rot = jnp.sum(onehot[:, :, None] * rotations[None], axis=1)]
    unnamed x14 -> x24, local copies, waits for them, and re-layouts: 2.87 us -> 5.63 us
    pallas_call x0 -> x1, Pallas kernels: none -> 1.89 us  [body(): pl.pallas_call(lambda *refs: tables_kernel(slots, *refs), out_shape=(jax....]
    pallas_call x1, Pallas kernels: 4.63 us -> 5.41 us  [body(): pl.pallas_call(lambda *refs: finish_kernel(slots, *refs), out_shape=jax.S...]
    broadcast_in_dim x1 -> x0, local copies, waits for them, and re-layouts: 0.75 us -> none  [body(): bias[:, None]]
    convert_element_type x1 -> x0, other arithmetic: 0.73 us -> none  [slot_tables(): onehot = (tile_map[:, None] == places[None, :]).astype(jnp.int32)]
where the time goes in v5:
time: 54.2 us; the launch traced here: 53.6 us
  Pallas kernels  44.9 us (83%)
  local copies, waits for them, and re-layouts  7.91 us (15%)
  between operations  0.74 us (1%)
    pallas_call x1, Pallas kernels, body(): pl.pallas_call(lambda *refs: gather_kernel(tile_size, *refs), grid=(back_...  13.3 us
    pallas_call x1, Pallas kernels, body(): pl.pallas_call(lambda *refs: sum_kernel(dp_size, tile_size, factor, *refs...  13.2 us
    pallas_call x1, Pallas kernels, body(): pl.pallas_call(lambda *refs: front_kernel(slots, *refs), grid_spec=pltpu....  11.1 us
    unnamed x24, local copies, waits for them, and re-layouts  5.63 us
    pallas_call x1, Pallas kernels, body(): pl.pallas_call(lambda *refs: finish_kernel(slots, *refs), out_shape=jax.S...  5.41 us
    pallas_call x1, Pallas kernels, body(): pl.pallas_call(lambda *refs: tables_kernel(slots, *refs), out_shape=(jax....  1.89 us

profile of v5, /device:TPU:0, one launch (start us, length us, event | category | flops | bytes accessed | tf_op | source)
XLA Modules:
  0.0 53.6 jit_solution(3785709771108666534)
XLA Ops:
  0.6 1.4 %copy.19.refs_1_ = s32[48,8]{1,0:T(8,128)} copy(s32[48,8]{0,1:T(8,128)} %param.15) | data formatting | bytes 3072 | tf_op args[4]
  2.0 1.4 %copy.20.refs_2_ = s32[48,8]{1,0:T(8,128)} copy(s32[48,8]{0,1:T(8,128)} %param.16) | data formatting | bytes 3072 | tf_op args[5]
  3.4 1.9 %tables.1 = (s32[48,8]{1,0:T(8,128)}, s32[48,8]{1,0:T(8,128)}, s32[48,8]{1,0:T(8,128)}) custom-call(s32[1,48]{1,0:T(1,128)} %bitcast.25, s32[48,8]{1,0:T(8,128)} %copy.19.refs_1_, s32[48,8]{1,0:T(8,128)} %copy.20.refs_2_), custom_call_target="tpu_custom_call" | custom-call | tf_op jit(solution)/shard_map/tables/pallas_call | solution.py:488
  5.3 0.0 copy-start.5
  5.3 0.0 copy-start.6
  5.3 0.9 %copy.21.refs_6_ = bf16[64,144]{1,0:T(8,128)(2,1)S(1)} copy(bf16[64,144]{0,1:T(8,128)(2,1)} %bitcast.19) | data formatting | bytes 36864 | tf_op jit(solution)/shard_map/reshape | solution.py:496
  6.1 0.0 copy-start
  6.2 1.1 %copy-done = bf16[1,24,16,1024]{3,2,1,0:T(8,128)(2,1)S(1)} copy-done((bf16[1,24,16,1024]{3,2,1,0:T(8,128)(2,1)S(1)}, bf16[1,24,16,1024]{3,2,1,0:T(8,128)(2,1)}, u32[]{:S(2)}) %copy-start) | copy-done | bytes 786456
  7.3 0.0 copy-start.2
  7.3 0.9 %copy-done.2 = bf16[1024,128]{1,0:T(8,128)(2,1)S(1)} copy-done((bf16[1024,128]{1,0:T(8,128)(2,1)S(1)}, bf16[1024,128]{1,0:T(8,128)(2,1)}, u32[]{:S(2)}) %copy-start.2) | copy-done | bytes 262168
  8.2 0.0 copy-start.3
  8.2 0.8 %copy-done.3 = bf16[64,16,3,3]{0,1,3,2:T(8,128)(2,1)S(1)} copy-done((bf16[64,16,3,3]{0,1,3,2:T(8,128)(2,1)S(1)}, bf16[64,16,3,3]{0,1,3,2:T(8,128)(2,1)}, u32[]{:S(2)}) %copy-start.3) | copy-done | bytes 18456
  9.0 0.0 copy-start.9
  9.0 0.0 copy-start.10
  9.0 13.3 %back.1 = (f32[24,16,1024]{2,1,0:T(8,128)S(1)}, bf16[48,16,128]{2,1,0:T(8,128)(2,1)S(1)}, bf16[48,16,256]{2,1,0:T(8,128)(2,1)S(1)}) custom-call(bf16[24,16,1024]{2,1,0:T(8,128)(2,1)S(1)} %bitcast.16, bf16[24,64,1024]{2,1,0:T(8,128)(2,1)} %bitcast.22, bf16[144,64]{1,0:T(8,128)(2,1)S(1)} %bitcast.20, bf16[1024,128]{1,0:T(8,128)(2,1)S(1)} %copy-done.2), custom_call_target="tpu_custom_call" | custom-call | tf_op jit(solution)/shard_map/back/pallas_call | solution.py:455
  22.3 0.0 copy-done.5
  22.3 0.0 copy-done.6
  22.3 0.0 copy-done.9
  22.3 0.0 copy-done.10
  22.3 0.0 copy-start.1
  22.4 0.0 copy-start.4
  22.4 0.0 copy-start.7
  22.4 0.0 copy-start.8
  22.4 5.4 %finish.1 = bf16[24,16,1024]{2,1,0:T(8,128)(2,1)} custom-call(s32[48,8]{1,0:T(8,128)S(1)} %copy-done.5, s32[48,8]{1,0:T(8,128)S(1)} %copy-done.6, bf16[48,16,256]{2,1,0:T(8,128)(2,1)S(1)} %get-tuple-element.17.refs_2_, bf16[128,1024]{1,0:T(8,128)(2,1)S(1)} %copy-done.10, bf16[256,1024]{1,0:T(8,128)(2,1)S(1)} %copy-done.9, ...), custom_call_target="tpu_custom_call" | custom-call | flops 3623878656 | bytes 6291456 | tf_op jit(solution)/shard_map/finish/pallas_call | solution.py:560
  27.8 0.0 copy-done.1
  27.8 0.0 copy-done.4
  27.8 0.0 copy-done.7
  27.8 0.0 copy-done.8
  27.8 11.1 %front.1 = (bf16[24,64,1024]{2,1,0:T(8,128)(2,1)}, f32[64,160]{1,0:T(8,128)S(1)}) custom-call(s32[48,8]{1,0:T(8,128)S(1)} %copy-done.4, bf16[48,16,128]{2,1,0:T(8,128)(2,1)S(1)} %get-tuple-element.13.refs_1_, bf16[128,1024]{1,0:T(8,128)(2,1)S(1)} %copy-done.10, bf16[256,1408]{1,0:T(8,128)(2,1)S(1)} %copy-done.8, bf16[24,16,1024]{2,1,0:T(8,128)(2,1)S(1)} %bitcast.17, ...), custom_call_target="tpu_custom_call" | custom-call | flops 7247757312 | bytes 6291456 | tf_op jit(solution)/shard_map/front/pallas_call | solution.py:498
  38.9 13.2 %sums.1 = f32[64,160]{1,0:T(8,128)S(1)} custom-call(f32[64,160]{1,0:T(8,128)S(1)} %get-tuple-element.19.refs_0_), custom_call_target="tpu_custom_call" | custom-call | tf_op jit(solution)/shard_map/sums/pallas_call | solution.py:534
  52.1 0.7 %slice_reduce_fusion = f32[64]{0:T(128)} fusion(f32[64,160]{1,0:T(8,128)S(1)} %sums.1), kind=kLoop, calls=%fused_computation | loop fusion | bytes 512 | tf_op jit(solution)/shard_map/slice | solution.py:557
  52.8 0.7 %copy.22 = f32[64,144]{0,1:T(8,128)} copy(f32[64,144]{1,0:T(8,128)S(1)} %bitcast.18) | data formatting | bytes 73728 | tf_op jit(solution)/shard_map/slice | solution.py:556
Async XLA Ops:
  5.3 17.0 %copy-start.5 = (s32[48,8]{1,0:T(8,128)S(1)}, s32[48,8]{1,0:T(8,128)}, u32[]{:S(2)}) copy-start(s32[48,8]{1,0:T(8,128)} %get-tuple-element.15.refs_0_) | copy-start | bytes 4612
  5.3 17.0 %copy-start.6 = (s32[48,8]{1,0:T(8,128)S(1)}, s32[48,8]{1,0:T(8,128)}, u32[]{:S(2)}) copy-start(s32[48,8]{1,0:T(8,128)} %get-tuple-element.16.refs_1_) | copy-start | bytes 4612
  6.1 1.1 %copy-start = (bf16[1,24,16,1024]{3,2,1,0:T(8,128)(2,1)S(1)}, bf16[1,24,16,1024]{3,2,1,0:T(8,128)(2,1)}, u32[]{:S(2)}) copy-start(bf16[1,24,16,1024]{3,2,1,0:T(8,128)(2,1)} %param.11) | copy-start | bytes 2359300
  7.3 0.9 %copy-start.2 = (bf16[1024,128]{1,0:T(8,128)(2,1)S(1)}, bf16[1024,128]{1,0:T(8,128)(2,1)}, u32[]{:S(2)}) copy-start(bf16[1024,128]{1,0:T(8,128)(2,1)} %constant.8.clone.refs_3_) | copy-start | bytes 786436
  8.2 0.8 %copy-start.3 = (bf16[64,16,3,3]{0,1,3,2:T(8,128)(2,1)S(1)}, bf16[64,16,3,3]{0,1,3,2:T(8,128)(2,1)}, u32[]{:S(2)}) copy-start(bf16[64,16,3,3]{0,1,3,2:T(8,128)(2,1)} %param.12) | copy-start | bytes 55300
  9.0 13.3 %copy-start.9 = (bf16[256,1024]{1,0:T(8,128)(2,1)S(1)}, bf16[256,1024]{1,0:T(8,128)(2,1)}, u32[]{:S(2)}) copy-start(bf16[256,1024]{1,0:T(8,128)(2,1)} %constant.11.clone.refs_4_) | copy-start | bytes 1572868
  9.0 13.3 %copy-start.10 = (bf16[128,1024]{1,0:T(8,128)(2,1)S(1)}, bf16[128,1024]{1,0:T(8,128)(2,1)}, u32[]{:S(2)}) copy-start(bf16[128,1024]{1,0:T(8,128)(2,1)} %constant.9.clone.refs_2_.refs_3_) | copy-start | bytes 786436
  22.3 5.5 %copy-start.1 = (bf16[1,24,16,1024]{3,2,1,0:T(8,128)(2,1)S(1)}, bf16[1,24,16,1024]{3,2,1,0:T(8,128)(2,1)}, u32[]{:S(2)}) copy-start(bf16[1,24,16,1024]{3,2,1,0:T(8,128)(2,1)} %param.11) | copy-start | bytes 2359300
  22.4 5.5 %copy-start.4 = (s32[48,8]{1,0:T(8,128)S(1)}, s32[48,8]{1,0:T(8,128)}, u32[]{:S(2)}) copy-start(s32[48,8]{1,0:T(8,128)} %get-tuple-element.12.refs_0_) | copy-start | bytes 4612
  22.4 5.4 %copy-start.7 = (f32[64]{0:T(128)S(1)}, f32[64]{0:T(128)}, u32[]{:S(2)}) copy-start(f32[64]{0:T(128)} %param.13) | copy-start | bytes 772
  22.4 5.4 %copy-start.8 = (bf16[256,1408]{1,0:T(8,128)(2,1)S(1)}, bf16[256,1408]{1,0:T(8,128)(2,1)}, u32[]{:S(2)}) copy-start(bf16[256,1408]{1,0:T(8,128)(2,1)} %constant.10.clone.refs_3_) | copy-start | bytes 2162692

commit v6 on v5

--- a/solution.py
+++ b/solution.py
@@ -48,8 +48,8 @@
     places = cols.astype(jnp.float32)
     held_col = jnp.sum(jnp.where(rows == cols, held, 0.0), axis=1, keepdims=True)
     onehot = jnp.where(held_col == places, 1.0, 0.0).astype(jnp.bfloat16)
-    tile_nbr = dot(onehot, nbr_ref[...].astype(jnp.float32).astype(jnp.bfloat16))
-    tile_rot = dot(onehot, rot_ref[...].astype(jnp.float32).astype(jnp.bfloat16))
+    tile_nbr = dot_last(onehot, nbr_ref[...].astype(jnp.float32).astype(jnp.bfloat16))
+    tile_rot = dot_last(onehot, rot_ref[...].astype(jnp.float32).astype(jnp.bfloat16))
     k_ids = lax.broadcasted_iota(jnp.int32, (total, 8), 1)
     s_ids = lax.broadcasted_iota(jnp.int32, (total, 8), 0)
     nbr = jnp.zeros((total, 8), jnp.float32)
@@ -123,6 +123,10 @@
 
 def dot(a, b):
     return jnp.dot(a, b, preferred_element_type=jnp.float32)
+
+
+def dot_last(a, b):
+    return lax.dot_general(a, b, (((1,), (1,)), ((), ())), preferred_element_type=jnp.float32)
 
 
 def lane_ids(width):
@@ -491,7 +495,7 @@
         in_specs=[vmem] * 3,
         out_specs=(vmem,) * 3,
         name="tables",
-    )(tile_map.reshape(1, total), neighbours, rotations)
+    )(tile_map.reshape(1, total), neighbours.T, rotations.T)
 
     wf = weights.transpose(0, 2, 3, 1).reshape(out_chans, 9 * in_chans)
     images = const(rim_images())

time: 54.2 us -> 51.4 us (0.948)
  local copies, waits for them, and re-layouts: 7.91 us -> 5.17 us
    unnamed x24 -> x22, local copies, waits for them, and re-layouts: 5.63 us -> 2.89 us
where the time goes in v6:
time: 51.4 us; the launch traced here: 50.8 us
  Pallas kernels  44.9 us (87%)
  local copies, waits for them, and re-layouts  5.17 us (10%)
  between operations  0.74 us (1%)
    pallas_call x1, Pallas kernels, body(): pl.pallas_call(lambda *refs: gather_kernel(tile_size, *refs), grid=(back_...  13.3 us
    pallas_call x1, Pallas kernels, body(): pl.pallas_call(lambda *refs: sum_kernel(dp_size, tile_size, factor, *refs...  13.2 us
    pallas_call x1, Pallas kernels, body(): pl.pallas_call(lambda *refs: front_kernel(slots, *refs), grid_spec=pltpu....  11.1 us
    pallas_call x1, Pallas kernels, body(): pl.pallas_call(lambda *refs: finish_kernel(slots, *refs), out_shape=jax.S...  5.41 us
    unnamed x22, local copies, waits for them, and re-layouts  2.89 us
    pallas_call x1, Pallas kernels, body(): pl.pallas_call(lambda *refs: tables_kernel(slots, *refs), out_shape=(jax....  1.84 us

profile of v6, /device:TPU:0, one launch (start us, length us, event | category | flops | bytes accessed | tf_op | source)
XLA Modules:
  0.0 50.8 jit_solution(2007463206291694881)
XLA Ops:
  0.6 0.9 %copy.17.refs_6_ = bf16[64,144]{1,0:T(8,128)(2,1)S(1)} copy(bf16[64,144]{0,1:T(8,128)(2,1)} %bitcast.21) | data formatting | bytes 36864 | tf_op jit(solution)/shard_map/reshape | solution.py:500
  1.5 1.8 %tables.1 = (s32[48,8]{1,0:T(8,128)}, s32[48,8]{1,0:T(8,128)}, s32[48,8]{1,0:T(8,128)}) custom-call(s32[1,48]{1,0:T(1,128)} %bitcast.29, s32[8,48]{1,0:T(8,128)} %bitcast.27, s32[8,48]{1,0:T(8,128)} %bitcast.28), custom_call_target="tpu_custom_call" | custom-call | tf_op jit(solution)/shard_map/tables/pallas_call | solution.py:492
  3.3 0.0 copy-start
  3.3 1.1 %copy-done = bf16[1,24,16,1024]{3,2,1,0:T(8,128)(2,1)S(1)} copy-done((bf16[1,24,16,1024]{3,2,1,0:T(8,128)(2,1)S(1)}, bf16[1,24,16,1024]{3,2,1,0:T(8,128)(2,1)}, u32[]{:S(2)}) %copy-start) | copy-done | bytes 786456
  4.5 0.0 copy-start.2
  4.5 0.9 %copy-done.2 = bf16[1024,128]{1,0:T(8,128)(2,1)S(1)} copy-done((bf16[1024,128]{1,0:T(8,128)(2,1)S(1)}, bf16[1024,128]{1,0:T(8,128)(2,1)}, u32[]{:S(2)}) %copy-start.2) | copy-done | bytes 262168
  5.4 0.0 copy-start.3
  5.4 0.8 %copy-done.3 = bf16[64,16,3,3]{0,1,3,2:T(8,128)(2,1)S(1)} copy-done((bf16[64,16,3,3]{0,1,3,2:T(8,128)(2,1)S(1)}, bf16[64,16,3,3]{0,1,3,2:T(8,128)(2,1)}, u32[]{:S(2)}) %copy-start.3) | copy-done | bytes 18456
  6.2 0.0 copy-start.5
  6.2 0.0 copy-start.6
  6.2 0.0 copy-start.9
  6.2 0.0 copy-start.10
  6.2 13.3 %back.1 = (f32[24,16,1024]{2,1,0:T(8,128)S(1)}, bf16[48,16,128]{2,1,0:T(8,128)(2,1)S(1)}, bf16[48,16,256]{2,1,0:T(8,128)(2,1)S(1)}) custom-call(bf16[24,16,1024]{2,1,0:T(8,128)(2,1)S(1)} %bitcast.18, bf16[24,64,1024]{2,1,0:T(8,128)(2,1)} %bitcast.24, bf16[144,64]{1,0:T(8,128)(2,1)S(1)} %bitcast.22, bf16[1024,128]{1,0:T(8,128)(2,1)S(1)} %copy-done.2), custom_call_target="tpu_custom_call" | custom-call | tf_op jit(solution)/shard_map/back/pallas_call | solution.py:459
  19.5 0.0 copy-done.5
  19.5 0.0 copy-done.6
  19.5 0.0 copy-done.9
  19.6 0.0 copy-done.10
  19.6 0.0 copy-start.1
  19.6 0.0 copy-start.4
  19.6 0.0 copy-start.7
  19.6 0.0 copy-start.8
  19.6 5.4 %finish.1 = bf16[24,16,1024]{2,1,0:T(8,128)(2,1)} custom-call(s32[48,8]{1,0:T(8,128)S(1)} %copy-done.5, s32[48,8]{1,0:T(8,128)S(1)} %copy-done.6, bf16[48,16,256]{2,1,0:T(8,128)(2,1)S(1)} %get-tuple-element.17.refs_2_, bf16[128,1024]{1,0:T(8,128)(2,1)S(1)} %copy-done.10, bf16[256,1024]{1,0:T(8,128)(2,1)S(1)} %copy-done.9, ...), custom_call_target="tpu_custom_call" | custom-call | flops 3623878656 | bytes 6291456 | tf_op jit(solution)/shard_map/finish/pallas_call | solution.py:564
  25.0 0.0 copy-done.1
  25.0 0.0 copy-done.4
  25.0 0.0 copy-done.7
  25.0 0.0 copy-done.8
  25.0 11.1 %front.1 = (bf16[24,64,1024]{2,1,0:T(8,128)(2,1)}, f32[64,160]{1,0:T(8,128)S(1)}) custom-call(s32[48,8]{1,0:T(8,128)S(1)} %copy-done.4, bf16[48,16,128]{2,1,0:T(8,128)(2,1)S(1)} %get-tuple-element.13.refs_1_, bf16[128,1024]{1,0:T(8,128)(2,1)S(1)} %copy-done.10, bf16[256,1408]{1,0:T(8,128)(2,1)S(1)} %copy-done.8, bf16[24,16,1024]{2,1,0:T(8,128)(2,1)S(1)} %bitcast.19, ...), custom_call_target="tpu_custom_call" | custom-call | flops 7247757312 | bytes 6291456 | tf_op jit(solution)/shard_map/front/pallas_call | solution.py:502
  36.1 13.2 %sums.1 = f32[64,160]{1,0:T(8,128)S(1)} custom-call(f32[64,160]{1,0:T(8,128)S(1)} %get-tuple-element.19.refs_0_), custom_call_target="tpu_custom_call" | custom-call | tf_op jit(solution)/shard_map/sums/pallas_call | solution.py:538
  49.4 0.7 %slice_reduce_fusion = f32[64]{0:T(128)} fusion(f32[64,160]{1,0:T(8,128)S(1)} %sums.1), kind=kLoop, calls=%fused_computation | loop fusion | bytes 512 | tf_op jit(solution)/shard_map/slice | solution.py:561
  50.1 0.7 %copy.18 = f32[64,144]{0,1:T(8,128)} copy(f32[64,144]{1,0:T(8,128)S(1)} %bitcast.20) | data formatting | bytes 73728 | tf_op jit(solution)/shard_map/slice | solution.py:560
Async XLA Ops:
  3.3 1.1 %copy-start = (bf16[1,24,16,1024]{3,2,1,0:T(8,128)(2,1)S(1)}, bf16[1,24,16,1024]{3,2,1,0:T(8,128)(2,1)}, u32[]{:S(2)}) copy-start(bf16[1,24,16,1024]{3,2,1,0:T(8,128)(2,1)} %param.11) | copy-start | bytes 2359300
  4.5 0.9 %copy-start.2 = (bf16[1024,128]{1,0:T(8,128)(2,1)S(1)}, bf16[1024,128]{1,0:T(8,128)(2,1)}, u32[]{:S(2)}) copy-start(bf16[1024,128]{1,0:T(8,128)(2,1)} %constant.8.clone.refs_3_) | copy-start | bytes 786436
  5.4 0.8 %copy-start.3 = (bf16[64,16,3,3]{0,1,3,2:T(8,128)(2,1)S(1)}, bf16[64,16,3,3]{0,1,3,2:T(8,128)(2,1)}, u32[]{:S(2)}) copy-start(bf16[64,16,3,3]{0,1,3,2:T(8,128)(2,1)} %param.12) | copy-start | bytes 55300
  6.2 13.3 %copy-start.5 = (s32[48,8]{1,0:T(8,128)S(1)}, s32[48,8]{1,0:T(8,128)}, u32[]{:S(2)}) copy-start(s32[48,8]{1,0:T(8,128)} %get-tuple-element.15.refs_0_) | copy-start | bytes 4612
  6.2 13.4 %copy-start.6 = (s32[48,8]{1,0:T(8,128)S(1)}, s32[48,8]{1,0:T(8,128)}, u32[]{:S(2)}) copy-start(s32[48,8]{1,0:T(8,128)} %get-tuple-element.16.refs_1_) | copy-start | bytes 4612
  6.2 13.4 %copy-start.9 = (bf16[256,1024]{1,0:T(8,128)(2,1)S(1)}, bf16[256,1024]{1,0:T(8,128)(2,1)}, u32[]{:S(2)}) copy-start(bf16[256,1024]{1,0:T(8,128)(2,1)} %constant.11.clone.refs_4_) | copy-start | bytes 1572868
  6.2 13.4 %copy-start.10 = (bf16[128,1024]{1,0:T(8,128)(2,1)S(1)}, bf16[128,1024]{1,0:T(8,128)(2,1)}, u32[]{:S(2)}) copy-start(bf16[128,1024]{1,0:T(8,128)(2,1)} %constant.9.clone.refs_2_.refs_3_) | copy-start | bytes 786436
  19.6 5.5 %copy-start.1 = (bf16[1,24,16,1024]{3,2,1,0:T(8,128)(2,1)S(1)}, bf16[1,24,16,1024]{3,2,1,0:T(8,128)(2,1)}, u32[]{:S(2)}) copy-start(bf16[1,24,16,1024]{3,2,1,0:T(8,128)(2,1)} %param.11) | copy-start | bytes 2359300
  19.6 5.5 %copy-start.4 = (s32[48,8]{1,0:T(8,128)S(1)}, s32[48,8]{1,0:T(8,128)}, u32[]{:S(2)}) copy-start(s32[48,8]{1,0:T(8,128)} %get-tuple-element.12.refs_0_) | copy-start | bytes 4612
  19.6 5.4 %copy-start.7 = (f32[64]{0:T(128)S(1)}, f32[64]{0:T(128)}, u32[]{:S(2)}) copy-start(f32[64]{0:T(128)} %param.13) | copy-start | bytes 772
  19.6 5.4 %copy-start.8 = (bf16[256,1408]{1,0:T(8,128)(2,1)S(1)}, bf16[256,1408]{1,0:T(8,128)(2,1)}, u32[]{:S(2)}) copy-start(bf16[256,1408]{1,0:T(8,128)(2,1)} %constant.10.clone.refs_3_) | copy-start | bytes 2162692
